TPU v7x, 32 devices: a whole 2x2x4 slice. The times are simulated.
32 devices in a mesh: ctx: 8 (over z, x), tp: 4 (over y, core).
Axes of the slice: x: 2, y: 2, z: 4, core: 2. Of those that a mesh axis runs over, the one named last changes fastest.
Arguments:
- x_raw: bfloat16 [1024, 4096], P('ctx', 'tp'), may hold values from -6 to 6
- b_raw: bfloat16 [1024, 512], P('ctx'), may hold values from -0.59765625 to 0.59765625
- c_raw: bfloat16 [1024, 512], P('ctx'), may hold values from -0.59765625 to 0.59765625
- z_gate: bfloat16 [1024, 4096], P('ctx', 'tp'), may hold values from -6 to 6
- dt_raw: float32 [1024, 128], P('ctx', 'tp'), may hold values from -4 to 4
- conv_x: float32 [4, 4096], P(None, 'tp'), may hold values from -3 to 3
- conv_b: float32 [4, 512], replicated, may hold values from -3 to 3
- conv_c: float32 [4, 512], replicated, may hold values from -3 to 3
- dt_bias: float32 [128], P('tp'), may hold values from -1 to 1
- a_log: float32 [128], P('tp'), may hold values from -14 to -3
- d_skip: float32 [128], P('tp'), may hold values from 0.5 to 1.5
- gain: float32 [4096], P('tp'), may hold values from 0.5 to 1.5
- grad_out: bfloat16 [1024, 4096], P('ctx', 'tp'), may hold values from -6 to 6
Outputs:
- grad_x_raw: bfloat16 [1024, 4096], P('ctx', 'tp')
- grad_b_raw: bfloat16 [1024, 512], P('ctx')
- grad_c_raw: bfloat16 [1024, 512], P('ctx')
- grad_z_gate: bfloat16 [1024, 4096], P('ctx', 'tp')
- grad_dt_raw: float32 [1024, 128], P('ctx', 'tp')
- grad_conv_x: float32 [4, 4096], P(None, 'tp')
- grad_conv_b: float32 [4, 512], replicated
- grad_conv_c: float32 [4, 512], replicated
- grad_dt_bias: float32 [128], P('tp')
- grad_a_log: float32 [128], P('tp')
- grad_d_skip: float32 [128], P('tp')
- grad_gain: float32 [4096], P('tp')
All inputs are finite; a program needn't handle non-finite values.
Results may differ from a plain program's by a relative error of at most 0.00105.
Values may be sent and summed in bfloat16 or wider, within the bound.
A program may use at most 192 MiB of HBM per device.

v0:
```python
import jax
import jax.numpy as jnp
from jax import lax
from jax.sharding import PartitionSpec as P

HEADS = 128
HEAD_DIM = 32
STATE = 128
GROUPS = 4
CONV = 4
SPAN = 128


PRECISE = lax.Precision.HIGHEST
EPSILON = 1e-05


def from_behind(x, axis, by):
    peers = lax.axis_size(axis)
    pairs = [(i, i + by) for i in range(peers) if 0 <= i + by < peers]
    return lax.ppermute(x, axis, pairs)


def prefix(value, axis, join, neutral, backward):
    count, mine = (lax.axis_size(axis), lax.axis_index(axis))
    pieces = jax.tree.map(lambda part: lax.all_gather(part, axis), value)
    if backward:
        pieces = jax.tree.map(lambda part: part[::-1], pieces)
        mine = count - 1 - mine
    subtotal = jax.tree.map(
        lambda part, zero: jnp.full_like(part, 0) + jnp.asarray(zero, part.dtype), value, neutral
    )

    def lap(position, subtotal):
        longer = join(subtotal, jax.tree.map(lambda part: part[position], pieces))
        return jax.tree.map(lambda new, old: jnp.where(position < mine, new, old), longer, subtotal)

    return lax.fori_loop(0, count - 1, lap, subtotal)


def shifted_conv(extended, weight):
    tap_count = weight.shape[0]
    length = extended.shape[0] - tap_count + 1
    total = weight[0] * extended[0:length]
    for offset in range(1, tap_count):
        total = total + weight[offset] * extended[offset : offset + length]
    return jax.nn.silu(total)


def soft_step(raw_step, step_bias):
    return jax.nn.softplus(raw_step + step_bias)


def gate_product(ssd_out, gate_in):
    return ssd_out * jax.nn.silu(gate_in)


def span_output(x_blk, b_blk, c_blk, dt_blk, cum_decay, skip_gain, states):
    length = x_blk.shape[1]
    causal = jnp.arange(length)[:, None] >= jnp.arange(length)[None, :]
    pair_inner = jnp.einsum("cqgn,csgn->cgqs", c_blk, b_blk, precision=PRECISE)
    cum_cols = jnp.transpose(cum_decay, (0, 2, 3, 1))
    spread = cum_cols[..., :, None] - cum_cols[..., None, :]
    weights = jnp.where(causal, jnp.exp(jnp.where(causal, spread, 0.0)), 0.0)
    dt_cols = jnp.transpose(dt_blk, (0, 2, 3, 1))
    weights = weights * pair_inner[:, None] * dt_cols[..., None, :]
    diagonal = jnp.einsum("crgqs,csrgp->cqrgp", weights, x_blk, precision=PRECISE)
    carried = jnp.einsum("cqgn,crgpn->cqrgp", c_blk, states, precision=PRECISE)
    carried = carried * jnp.exp(cum_decay)[..., None]
    return diagonal + carried + skip_gain[:, :, None] * x_blk


def span_state(x_blk, b_blk, dt_blk, cum_decay):
    weight_rows = jnp.exp(cum_decay[:, -1:] - cum_decay) * dt_blk
    weighted = weight_rows[..., None] * x_blk
    return jnp.einsum("cqrgp,cqgn->crgpn", weighted, b_blk, precision=PRECISE)


def link_combine(earlier, later):
    return (later[0] * earlier[0], later[0][..., None, None] * earlier[1] + later[1])


def body(
    x_raw,
    b_raw,
    c_raw,
    z_gate,
    dt_raw,
    conv_x,
    conv_b,
    conv_c,
    dt_bias,
    a_log,
    d_skip,
    gain,
    grad_out,
):
    rows = x_raw.shape[0]
    halo_rows = CONV - 1
    per_local = x_raw.shape[1] // HEAD_DIM // GROUPS
    blocks_here = rows // SPAN
    group_width = HEADS // GROUPS * HEAD_DIM
    tails = (x_raw[rows - halo_rows :], b_raw[rows - halo_rows :], c_raw[rows - halo_rows :])
    before = from_behind((tails[0], tails[1], tails[2]), "ctx", 1)
    x_ext = jnp.concatenate([before[0], x_raw], axis=0).astype(jnp.float32)
    b_ext = jnp.concatenate([before[1], b_raw], axis=0).astype(jnp.float32)
    c_ext = jnp.concatenate([before[2], c_raw], axis=0).astype(jnp.float32)
    x_flat, x_conv_back = jax.vjp(shifted_conv, x_ext, conv_x)
    b_flat, b_conv_back = jax.vjp(shifted_conv, b_ext, conv_b)
    c_flat, c_conv_back = jax.vjp(shifted_conv, c_ext, conv_c)
    step_dt, step_back = jax.vjp(soft_step, dt_raw, dt_bias)

    def shaped(x_rows, b_rows, dt_rows, log_rate):
        x_blk = x_rows.reshape(blocks_here, SPAN, per_local, GROUPS, HEAD_DIM)
        b_blk = b_rows.reshape(blocks_here, SPAN, GROUPS, STATE)
        dt_blk = dt_rows.reshape(blocks_here, SPAN, per_local, GROUPS)
        decay_rate = jnp.exp(log_rate).reshape(per_local, GROUPS)
        cum_decay = jnp.cumsum(-decay_rate * dt_blk, axis=1)
        return (x_blk, b_blk, dt_blk, cum_decay)

    def summarize(x_rows, b_rows, dt_rows, log_rate):
        x_blk, b_blk, dt_blk, cum_decay = shaped(x_rows, b_rows, dt_rows, log_rate)
        own_states = span_state(x_blk, b_blk, dt_blk, cum_decay)
        block_ends = cum_decay[:, -1]

        def advance(carry_state, pieces):
            return (jnp.exp(pieces[0])[..., None, None] * carry_state + pieces[1], carry_state)

        initial = jnp.zeros(own_states.shape[1:], jnp.float32)
        finished, entering = lax.scan(advance, initial, (block_ends, own_states))
        return (entering, jnp.exp(jnp.sum(block_ends, axis=0)), finished)

    def produce(x_rows, b_rows, c_rows, dt_rows, log_rate, skip_rows, entering, enter_state):
        x_blk, b_blk, dt_blk, cum_decay = shaped(x_rows, b_rows, dt_rows, log_rate)
        c_blk = c_rows.reshape(blocks_here, SPAN, GROUPS, STATE)
        block_ends = cum_decay[:, -1]
        earlier = jnp.concatenate(
            [jnp.zeros_like(block_ends), jnp.cumsum(block_ends[:-1], axis=0)], axis=0
        )
        states = entering + jnp.exp(earlier)[..., None, None] * enter_state[None]
        skip_gain = skip_rows.reshape(per_local, GROUPS)
        result = span_output(x_blk, b_blk, c_blk, dt_blk, cum_decay, skip_gain, states)
        return result.reshape(rows, per_local * GROUPS * HEAD_DIM)

    def group_sums(values):
        return jnp.sum(values.reshape(rows, per_local, GROUPS, HEAD_DIM), axis=(1, 3))

    def spread_groups(values):
        return jnp.broadcast_to(
            values[:, None, :, None], (rows, per_local, GROUPS, HEAD_DIM)
        ).reshape(rows, -1)

    (entering, dev_decay, dev_state), summary_back = jax.vjp(
        summarize, x_flat, b_flat, step_dt, a_log
    )
    enter_state = prefix(
        (dev_decay, dev_state),
        "ctx",
        link_combine,
        (jnp.ones_like(dev_decay), jnp.zeros_like(dev_state)),
        False,
    )[1]
    ssd_out, produce_back = jax.vjp(
        produce, x_flat, b_flat, c_flat, step_dt, a_log, d_skip, entering, enter_state
    )
    gated_out, gate_back = jax.vjp(gate_product, ssd_out, z_gate.astype(jnp.float32))
    square_sums = lax.psum(group_sums(gated_out * gated_out), "tp")
    inverse = lax.rsqrt(square_sums / group_width + EPSILON)
    inverse_cols = spread_groups(inverse)
    out_grad = grad_out.astype(jnp.float32)
    gain_part = jnp.sum(out_grad * gated_out * inverse_cols, axis=0)
    gain_total = lax.psum(gain_part, "ctx")
    scaled_grad = out_grad * gain
    inner_total = lax.psum(group_sums(scaled_grad * gated_out), "tp")
    correction = spread_groups(inverse * inverse * inverse * inner_total / group_width)
    gated_grad = inverse_cols * scaled_grad - gated_out * correction
    ssd_grad, gate_grad = gate_back(gated_grad)
    (
        x_grad_one,
        b_grad_one,
        c_grad_part,
        step_grad_one,
        rate_grad_one,
        skip_grad,
        entering_grad,
        state_grad,
    ) = produce_back(ssd_grad)
    later_grad = prefix(
        (dev_decay, state_grad),
        "ctx",
        link_combine,
        (jnp.ones_like(dev_decay), jnp.zeros_like(state_grad)),
        True,
    )[1]
    decay_grad = jnp.sum(later_grad * enter_state, axis=(2, 3))
    x_grad_two, b_grad_two, step_grad_two, rate_grad_two = summary_back(
        (entering_grad, decay_grad, later_grad)
    )
    rate_grad = rate_grad_one + rate_grad_two
    raw_step_grad, bias_grad = step_back(step_grad_one + step_grad_two)
    bias_total, rate_total, skip_total = lax.psum((bias_grad, rate_grad, skip_grad), "ctx")
    b_grad, c_grad = lax.psum((b_grad_one + b_grad_two, c_grad_part), "tp")
    x_ext_grad, weight_x_grad = x_conv_back(x_grad_one + x_grad_two)
    b_ext_grad, weight_b_grad = b_conv_back(b_grad)
    c_ext_grad, weight_c_grad = c_conv_back(c_grad)
    returned = from_behind(
        (x_ext_grad[:halo_rows], b_ext_grad[:halo_rows], c_ext_grad[:halo_rows]), "ctx", -1
    )

    def settle(ext_grad, incoming):
        own_rows = ext_grad[halo_rows:]
        return jnp.concatenate(
            [own_rows[: rows - halo_rows], own_rows[rows - halo_rows :] + incoming], axis=0
        )

    grad_x_raw = settle(x_ext_grad, returned[0]).astype(jnp.bfloat16)
    grad_b_raw = settle(b_ext_grad, returned[1]).astype(jnp.bfloat16)
    grad_c_raw = settle(c_ext_grad, returned[2]).astype(jnp.bfloat16)
    conv_x_total, conv_b_total, conv_c_total = lax.psum(
        (weight_x_grad, weight_b_grad, weight_c_grad), "ctx"
    )
    return (
        grad_x_raw,
        grad_b_raw,
        grad_c_raw,
        gate_grad.astype(jnp.bfloat16),
        raw_step_grad,
        conv_x_total,
        conv_b_total,
        conv_c_total,
        bias_total,
        rate_total,
        skip_total,
        gain_total,
    )


def solution(mesh):
    return jax.shard_map(
        body,
        mesh=mesh,
        in_specs=(
            P("ctx", "tp"),
            P("ctx", None),
            P("ctx", None),
            P("ctx", "tp"),
            P("ctx", "tp"),
            P(None, "tp"),
            P(),
            P(),
            P("tp"),
            P("tp"),
            P("tp"),
            P("tp"),
            P("ctx", "tp"),
        ),
        out_specs=(
            P("ctx", "tp"),
            P("ctx", None),
            P("ctx", None),
            P("ctx", "tp"),
            P("ctx", "tp"),
            P(None, "tp"),
            P(),
            P(),
            P("tp"),
            P("tp"),
            P("tp"),
            P("tp"),
        ),
        check_vma=False,
    )
```

profile of v0, /device:TPU:0, one launch (start us, length us, event | category | flops | bytes accessed | tf_op | source)
XLA Modules:
  0.0 344.4 jit_solution(9463993277914046449)
XLA Ops:
  8.3 4.9 %collective-permute-start = (bf16[3,1024]{0,1:T(8,128)(2,1)S(1)}, bf16[3,1024]{0,1:T(8,128)(2,1)S(1)}, u32[]{:S(2)}, u32[]{:S(2)}) collective-permute-start(bf16[3,1024]{0,1:T(8,128)(2,1)S(1)} %copy.311), channel_id=1, source_target_pairs={{0,4},{4,8},{8,12},{12,16},{16,20},{20,24},{24,28},{1,5},{5,9},{9,... | collective-permute-start | bytes 18440 | tf_op jit(solution)/shard_map/ppermute | solution.py:21
  13.9 3.4 collective-permute-start.2
  24.7 2.6 fusion.65
  28.9 1.3 slice.134
  30.2 4.0 %collective-permute-start.1 = (bf16[3,512]{1,0:T(4,128)(2,1)}, bf16[3,512]{1,0:T(4,128)(2,1)}, u32[]{:S(2)}, u32[]{:S(2)}) collective-permute-start(bf16[3,512]{1,0:T(4,128)(2,1)} %slice.134), channel_id=1, source_target_pairs={{0,4},{4,8},{8,12},{12,16},{16,20},{20,24},{24,28},{1,5},{5,9},{9,... | collective-permute-start | bytes 9224 | tf_op jit(solution)/shard_map/ppermute | solution.py:21
  39.4 27.1 %all-gather = f32[8,1,8,4]{2,3,1,0:T(4,128)} all-gather(f32[1,1,8,4]{2,3,1,0:T(4,128)S(1)} %copy.320), channel_id=2, replica_groups=mesh['ctx'=8,'tp'=4] {'ctx'}, dimensions={0}, use_global_device_ids=true | all-gather | bytes 1152 | tf_op jit(solution)/shard_map/all_gather | solution.py:26
  67.4 1.5 fusion.79
  71.6 1.4 fusion.72
  73.0 29.9 %all-gather.4.cloned.1.call-done = f32[8,8,4,32,128]{4,3,2,1,0:T(8,128)} async-done(((f32[1,8,4,32,128]{4,3,2,1,0:T(8,128)}), f32[8,8,4,32,128]{4,3,2,1,0:T(8,128)}) %all-gather.4.cloned.1.call-update) | async-done | bytes 4194320 | tf_op jit(solution)/shard_map/all_gather | solution.py:26
  102.9 13.5 %while.18 = (s32[]{:T(128)}, f32[8,4,32,128]{3,2,1,0:T(8,128)S(1)}, s32[]{:T(128)}, f32[8,8,4]{1,2,0:T(4,128)}, f32[8,8,4,32,128]{4,3,2,1,0:T(8,128)}, /*index=5*/s32[]{:T(128)}, s32[]{:T(128)}) while((s32[]{:T(128)}, f32[8,4,32,128]{3,2,1,0:T(8,128)S(1)}, s32[]{:T(128)}, f32[8,8,4]{1,2,0:T(4,128)}, ...), condition=%wide.region_2.3_spmd.clone, body=%wide.region_1.2_spmd.clone.sunk | while | flops 524292 | bytes 1573609 | solution.py:38
  117.1 4.8 %fusion.25 = f32[1,128,8,4,32]{1,4,3,2,0:T(8,128)S(1)} fusion(f32[128,8,4,32]{0,3,2,1:T(8,128)S(1)} %bitcast.275, f32[8,4,128]{2,1,0:T(4,128)S(1)} %bitcast.292, f32[4,128,128]{2,1,0:T(8,128)} %fusion.72, f32[8,4,128]{2,1,0:T(4,128)} %copy.316, pred[128,128]{1,0:T(8,128)(4,1)} %iota_compare_fusion, f32[1,128,8,4,32]{1,4,3,2,0:T(8,128)S(1)} %bitcast.276, ...), kind=kOutput, calls=%fused_computation.25 | convolution fusion | flops 204472320 | bytes 2424960 | tf_op jit(solution)/shard_map/jvp(crgqs,csrgp->cqrgp)/dot_general | solution.py:67
  123.1 1.7 reduce_sum.281
  124.8 1.7 reduce_sum.282
  126.5 6.4 %all-reduce.27 = (f32[128,4]{0,1:T(4,128)}, f32[128,4]{0,1:T(4,128)}) all-reduce(f32[128,4]{0,1:T(4,128)} %reduce_sum.282, f32[128,4]{0,1:T(4,128)} %reduce_sum.281), channel_id=1, replica_groups=mesh['ctx'=8,'tp'=4] {'tp'}, use_global_device_ids=true, to_apply=%region_6.7 | all-reduce | flops 1024 | bytes 8192 | tf_op jit(solution)/shard_map/psum | solution.py:174
  133.6 3.1 multiply_reduce_fusion.2
  139.2 1.3 rev.6
  142.0 1.3 copy.360
  144.1 1.4 multiply_reduce_fusion.10
  145.5 6.9 %fusion.30 = (f32[8,4,128]{2,1,0:T(4,128)S(1)}, f32[8,4,128]{2,1,0:T(4,128)S(1)}, f32[8,4,128]{2,1,0:T(4,128)}, f32[4,128,128]{2,1,0:T(8,128)}) fusion(f32[8,4,128]{2,1,0:T(4,128)S(1)} %bitcast.293, f32[4,128,128]{2,1,0:T(8,128)} %fusion.72, f32[8,4,128]{2,1,0:T(4,128)} %copy.316, pred[128,128]{1,0:T(8,128)(4,1)} %iota_compare_fusion, ...), kind=kOutput, calls=%fused_computation.32 | convolution fusion | flops 209113088 | bytes 1671168 | tf_op jit(solution)/shard_map/transpose(jvp(crgqs,csrgp->cqrgp))/dot_general | solution.py:67
  153.0 1.8 copy.351
  154.8 1.7 copy.346
  156.5 2.9 fusion.111
  159.4 1.8 copy.365
  161.3 2.0 bitcast_add_fusion.2
  163.3 1.8 copy.352
  165.1 1.4 copy.364
  166.6 1.4 copy.366
  168.0 2.1 convolution_bitcast_fusion.4
  170.1 2.3 convolution_add_fusion
  172.5 1.8 copy.345
  175.7 1.3 reshape.571
  177.0 1.8 copy.370
  178.8 2.2 convolution_bitcast_fusion.6
  181.1 30.0 %all-gather.6.cloned.1.call-done = f32[8,8,4,32,128]{4,3,2,1,0:T(8,128)} async-done(((f32[1,8,4,32,128]{4,3,2,1,0:T(8,128)}), f32[8,8,4,32,128]{4,3,2,1,0:T(8,128)}) %all-gather.6.cloned.1.call-update) | async-done | bytes 4194320 | tf_op jit(solution)/shard_map/all_gather | solution.py:26
  211.0 5.0 %rev.7 = f32[8,8,4,32,128]{4,3,2,1,0:T(8,128)} reverse(f32[8,8,4,32,128]{4,3,2,1,0:T(8,128)} %all-gather.6.cloned.1.call-done), dimensions={0} | reverse | bytes 8388608 | tf_op jit(solution)/shard_map/rev | solution.py:28
  216.0 13.6 %while.19 = (s32[]{:T(128)}, f32[8,4,32,128]{3,2,1,0:T(8,128)S(1)}, s32[]{:T(128)}, f32[8,8,4]{1,2,0:T(4,128)}, f32[8,8,4,32,128]{4,3,2,1,0:T(8,128)}, /*index=5*/s32[]{:T(128)}, s32[]{:T(128)}) while((s32[]{:T(128)}, f32[8,4,32,128]{3,2,1,0:T(8,128)S(1)}, s32[]{:T(128)}, f32[8,8,4]{1,2,0:T(4,128)}, ...), condition=%wide.region_8.9_spmd.clone, body=%wide.region_7.8_spmd.clone.sunk | while | flops 524292 | bytes 1573609 | solution.py:38
  230.5 2.5 multiply_reduce_fusion.9
  236.4 2.1 fusion.58
  240.5 2.6 reduce_window_sum.42
  243.1 1.8 fusion.28
  244.8 3.6 %fusion.19 = f32[1,128,8,4,32]{1,4,3,2,0:T(8,128)S(1)} fusion(f32[8,4,32,128]{3,2,1,0:T(8,128)S(1)} %bitcast.281, f32[8,4,128]{2,1,0:T(4,128)S(1)} %bitcast.294, f32[4,128,128]{2,1,0:T(8,128)} %fusion.72, f32[8,4,128]{2,1,0:T(4,128)} %copy.316, pred[128,128]{1,0:T(8,128)(4,1)} %iota_compare_fusion, f32[1,128,8,4,32]{1,4,3,2,0:T(8,128)} %get-tuple-element.476, ...), kind=kOutput, calls=%fused_computation.23 | convolution fusion | flops 204472320 | bytes 2424960 | tf_op jit(solution)/shard_map/transpose(jvp(crgqs,csrgp->cqrgp))/dot_general | solution.py:67
  251.2 1.3 collective-permute-start.3
  254.4 1.5 copy.371
  256.0 9.6 %collective-permute-done.3 = f32[3,1024]{0,1:T(8,128)S(1)} collective-permute-done((f32[3,1024]{0,1:T(8,128)S(1)}, f32[3,1024]{0,1:T(8,128)S(1)}, u32[]{:S(2)}, u32[]{:S(2)}) %collective-permute-start.3) | collective-permute-done | bytes 12320 | tf_op jit(solution)/shard_map/ppermute | solution.py:21
  266.7 23.0 %all-reduce.31.cloned.1.call-done = (f32[128,512]{1,0:T(8,128)}, f32[128,512]{1,0:T(8,128)}) async-done(((f32[128,512]{1,0:T(8,128)}, f32[128,512]{1,0:T(8,128)}), (f32[128,512]{1,0:T(8,128)}, f32[128,512]{1,0:T(8,128)})) %all-reduce.31.cloned.1.call-update) | async-done | bytes 524304 | tf_op jit(solution)/shard_map/psum | solution.py:202
  292.5 1.3 collective-permute-start.5
  293.8 1.3 collective-permute-start.4
  295.2 41.3 %all-reduce.26 = (f32[4,1024]{1,0:T(4,128)}, f32[4,512]{1,0:T(4,128)}, f32[4,512]{1,0:T(4,128)}, f32[32]{0:T(128)}, f32[32]{0:T(128)}, /*index=5*/f32[32]{0:T(128)}, f32[1024]{0:T(1024)}) all-reduce(f32[4,1024]{1,0:T(4,128)S(1)} %pad_add_fusion.3, f32[4,512]{1,0:T(4,128)S(1)} %pad_add_fusion.7, ...), channel_id=1, replica_groups=mesh['ctx'=8,'tp'=4] {'ctx'}, use_global_device_ids=true, to_apply=%region_26.27 | all-reduce | flops 9312 | bytes 74496 | tf_op jit(solution)/shard_map/psum | solution.py:219
  (268 shorter events, 71.4 us)
Async XLA Ops:
  7.2 16.0 %copy-start.20 = (bf16[128,1024]{1,0:T(8,128)(2,1)S(1)}, bf16[128,1024]{1,0:T(8,128)(2,1)}, u32[]{:S(2)}) copy-start(bf16[128,1024]{1,0:T(8,128)(2,1)} %param.17) | copy-start | bytes 786436
  7.2 16.3 %copy-start.31 = (bf16[128,512]{1,0:T(8,128)(2,1)S(1)}, bf16[128,512]{1,0:T(8,128)(2,1)}, u32[]{:S(2)}) copy-start(bf16[128,512]{1,0:T(8,128)(2,1)} %param.18) | copy-start | bytes 393220
  7.2 14.6 %copy-start.54 = (f32[4,1024]{1,0:T(4,128)S(1)}, f32[4,1024]{1,0:T(4,128)}, u32[]{:S(2)}) copy-start(f32[4,1024]{1,0:T(4,128)} %param.22) | copy-start | bytes 49156
  7.2 15.3 %copy-start.56 = (f32[4,512]{1,0:T(4,128)S(1)}, f32[4,512]{1,0:T(4,128)}, u32[]{:S(2)}) copy-start(f32[4,512]{1,0:T(4,128)} %param.23) | copy-start | bytes 24580
  7.2 95.7 %all-gather.4.cloned.1.call-start = ((), (), s32[]{:S(2)}) async-start(), calls=%async_computation | async-start | bytes 4718592 | tf_op jit(solution)/shard_map/all_gather | solution.py:26
  8.3 16.2 %collective-permute-start = (bf16[3,1024]{0,1:T(8,128)(2,1)S(1)}, bf16[3,1024]{0,1:T(8,128)(2,1)S(1)}, u32[]{:S(2)}, u32[]{:S(2)}) collective-permute-start(bf16[3,1024]{0,1:T(8,128)(2,1)S(1)} %copy.311), channel_id=1, source_target_pairs={{0,4},{4,8},{8,12},{12,16},{16,20},{20,24},{24,28},{1,5},{5,9},{9,... | collective-permute-start | bytes 18440 | tf_op jit(solution)/shard_map/ppermute | solution.py:21
  13.9 9.6 %collective-permute-start.2 = (bf16[3,512]{1,0:T(4,128)(2,1)S(1)}, bf16[3,512]{1,0:T(4,128)(2,1)S(1)}, u32[]{:S(2)}, u32[]{:S(2)}) collective-permute-start(bf16[3,512]{1,0:T(4,128)(2,1)S(1)} %slice.143), channel_id=1, source_target_pairs={{0,4},{4,8},{8,12},{12,16},{16,20},{20,24},{24,28},{1,5},{5,9},{9,... | collective-permute-start | bytes 9224 | tf_op jit(solution)/shard_map/ppermute | solution.py:21
  19.2 5.2 %copy-start.4 = (f32[1,128,8,4]{3,2,1,0:T(8,128)}, f32[1,128,8,4]{3,2,1,0:T(8,128)S(1)}, u32[]{:S(2)}) copy-start(f32[1,128,8,4]{3,2,1,0:T(8,128)S(1)} %copy.315) | copy-start | bytes 49156
  24.5 2.9 copy-start.55
  27.3 89.7 %copy-start = (f32[128,1024]{0,1:T(8,128)}, f32[128,1024]{0,1:T(8,128)S(1)}, u32[]{:S(2)}) copy-start(f32[128,1024]{0,1:T(8,128)S(1)} %get-tuple-element.437) | copy-start | bytes 1572868
  27.3 6.8 %copy-start.57 = (f32[4,512]{1,0:T(4,128)S(1)}, f32[4,512]{1,0:T(4,128)}, u32[]{:S(2)}) copy-start(f32[4,512]{1,0:T(4,128)} %param.24) | copy-start | bytes 24580
  27.3 8.1 %copy-start.53 = (f32[1,1,8,4]{3,2,1,0:T(8,128)S(1)}, f32[1,1,8,4]{3,2,1,0:T(8,128)}, u32[]{:S(2)}) copy-start(f32[1,1,8,4]{3,2,1,0:T(8,128)} %get-tuple-element.448) | copy-start | bytes 388
  27.3 10.3 %copy-start.25 = (bf16[128,1024]{1,0:T(8,128)(2,1)S(1)}, bf16[128,1024]{1,0:T(8,128)(2,1)}, u32[]{:S(2)}) copy-start(bf16[128,1024]{1,0:T(8,128)(2,1)} %param.20) | copy-start | bytes 786436
  27.3 11.1 %copy-start.26 = (bf16[128,1024]{1,0:T(8,128)(2,1)S(1)}, bf16[128,1024]{1,0:T(8,128)(2,1)}, u32[]{:S(2)}) copy-start(bf16[128,1024]{1,0:T(8,128)(2,1)} %param.29) | copy-start | bytes 786436
  28.8 182.2 %all-gather.6.cloned.1.call-start = ((), (), s32[]{:S(2)}) async-start(), calls=%async_computation.1 | async-start | bytes 4718592 | tf_op jit(solution)/shard_map/all_gather | solution.py:26
  30.2 36.3 %collective-permute-start.1 = (bf16[3,512]{1,0:T(4,128)(2,1)}, bf16[3,512]{1,0:T(4,128)(2,1)}, u32[]{:S(2)}, u32[]{:S(2)}) collective-permute-start(bf16[3,512]{1,0:T(4,128)(2,1)} %slice.134), channel_id=1, source_target_pairs={{0,4},{4,8},{8,12},{12,16},{16,20},{20,24},{24,28},{1,5},{5,9},{9,... | collective-permute-start | bytes 9224 | tf_op jit(solution)/shard_map/ppermute | solution.py:21
  37.6 79.4 %copy-start.60 = (f32[8,4]{1,0:T(8,128)}, f32[8,4]{1,0:T(8,128)S(1)}, u32[]{:S(2)}) copy-start(f32[8,4]{1,0:T(8,128)S(1)} %mul.694) | copy-start | bytes 388
  117.0 4.8 %copy-start.13 = (f32[1,128,8,4,32]{1,4,3,2,0:T(8,128)}, f32[1,128,8,4,32]{1,4,3,2,0:T(8,128)S(1)}, u32[]{:S(2)}) copy-start(f32[1,128,8,4,32]{1,4,3,2,0:T(8,128)S(1)} %convolution_bitcast_fusion.2) | copy-start | bytes 1572868
  117.0 4.8 %copy-start.11 = (bf16[128,1024]{0,1:T(8,128)(2,1)S(1)}, bf16[128,1024]{0,1:T(8,128)(2,1)}, u32[]{:S(2)}) copy-start(bf16[128,1024]{0,1:T(8,128)(2,1)} %copy.333) | copy-start | bytes 786436
  117.0 4.8 %copy-start.12 = (bf16[128,1024]{0,1:T(8,128)(2,1)S(1)}, bf16[128,1024]{0,1:T(8,128)(2,1)}, u32[]{:S(2)}) copy-start(bf16[128,1024]{0,1:T(8,128)(2,1)} %copy.334) | copy-start | bytes 786436
  117.0 4.8 %copy-start.51 = (f32[1024]{0:T(1024)S(1)}, f32[1024]{0:T(1024)}, u32[]{:S(2)}) copy-start(f32[1024]{0:T(1024)} %param.28) | copy-start | bytes 12292
  121.9 11.7 %copy-start.5 = (f32[128,1024]{0,1:T(8,128)S(1)}, f32[128,1024]{0,1:T(8,128)}, u32[]{:S(2)}) copy-start(f32[128,1024]{0,1:T(8,128)} %get-tuple-element.438) | copy-start | bytes 1572868
  123.1 14.4 %copy-start.29 = (f32[128,8,4]{0,2,1:T(4,128)S(1)}, f32[128,8,4]{0,2,1:T(4,128)}, u32[]{:S(2)}) copy-start(f32[128,8,4]{0,2,1:T(4,128)} %copy.332) | copy-start | bytes 49156
  132.8 4.6 %copy-start.17 = (f32[128,4,128]{2,1,0:T(4,128)S(1)}, f32[128,4,128]{2,1,0:T(4,128)}, u32[]{:S(2)}) copy-start(f32[128,4,128]{2,1,0:T(4,128)} %reshape.542) | copy-start | bytes 786436
  139.0 150.7 %all-reduce.31.cloned.1.call-start = ((), (), s32[]{:S(2)}) async-start(), calls=%async_computation.2 | async-start | bytes 1048576 | tf_op jit(solution)/shard_map/psum | solution.py:202
  145.5 6.9 %copy-start.28 = (f32[1,128,8,4]{1,2,3,0:T(8,128)S(1)}, f32[1,128,8,4]{1,2,3,0:T(8,128)}, u32[]{:S(2)}) copy-start(f32[1,128,8,4]{1,2,3,0:T(8,128)} %copy-done.27) | copy-start | bytes 49156
  154.8 13.3 %copy-start.30 = (f32[128,8,4]{0,2,1:T(4,128)S(1)}, f32[128,8,4]{0,2,1:T(4,128)}, u32[]{:S(2)}) copy-start(f32[128,8,4]{0,2,1:T(4,128)} %copy.332) | copy-start | bytes 49156
  216.0 14.5 %copy-start.8 = (f32[16,4,8,128]{3,2,1,0:T(8,128)S(1)}, f32[16,4,8,128]{3,2,1,0:T(8,128)}, u32[]{:S(2)}) copy-start(f32[16,4,8,128]{3,2,1,0:T(8,128)} %copy-done.7) | copy-start | bytes 786436
  232.9 10.2 %copy-start.1 = (f32[128,1024]{0,1:T(8,128)S(1)}, f32[128,1024]{0,1:T(8,128)}, u32[]{:S(2)}) copy-start(f32[128,1024]{0,1:T(8,128)} %copy-done) | copy-start | bytes 1572868
  232.9 10.2 %copy-start.15 = (f32[1,128,4,128]{1,3,2,0:T(8,128)S(1)}, f32[1,128,4,128]{1,3,2,0:T(8,128)}, u32[]{:S(2)}) copy-start(f32[1,128,4,128]{1,3,2,0:T(8,128)} %convolution_bitcast_fusion.6) | copy-start | bytes 786436
  238.5 6.3 %copy-start.3 = (f32[128,1024]{0,1:T(8,128)S(1)}, f32[128,1024]{0,1:T(8,128)}, u32[]{:S(2)}) copy-start(f32[128,1024]{0,1:T(8,128)} %copy-done.2) | copy-start | bytes 1572868
  244.8 3.6 %copy-start.6 = (f32[128,1024]{0,1:T(8,128)S(1)}, f32[128,1024]{0,1:T(8,128)}, u32[]{:S(2)}) copy-start(f32[128,1024]{0,1:T(8,128)} %get-tuple-element.438) | copy-start | bytes 1572868
  250.2 2.3 copy-start.18
  250.2 2.3 copy-start.19
  250.2 2.3 copy-start.22
  250.2 2.3 copy-start.23
  250.3 3.1 copy-start.64
  250.3 3.2 copy-start.16
  251.2 14.4 %collective-permute-start.3 = (f32[3,1024]{0,1:T(8,128)S(1)}, f32[3,1024]{0,1:T(8,128)S(1)}, u32[]{:S(2)}, u32[]{:S(2)}) collective-permute-start(f32[3,1024]{0,1:T(8,128)S(1)} %slice.176), channel_id=1, source_target_pairs={{4,0},{8,4},{12,8},{16,12},{20,16},{24,20},{28,24},{5,1},{9,5},{13... | collective-permute-start | bytes 36872 | tf_op jit(solution)/shard_map/ppermute | solution.py:21
  253.4 36.2 %copy-start.10 = (f32[128,512]{1,0:T(8,128)S(1)}, f32[128,512]{1,0:T(8,128)}, u32[]{:S(2)}) copy-start(f32[128,512]{1,0:T(8,128)} %get-tuple-element.434) | copy-start | bytes 786436
  255.9 34.9 %copy-start.47 = (f32[1,512]{1,0:T(1,128)S(1)}, f32[1,512]{1,0:T(1,128)}, u32[]{:S(2)}) copy-start(f32[1,512]{1,0:T(1,128)} %get-tuple-element.465) | copy-start | bytes 6148
  256.0 34.9 %copy-start.48 = (f32[1,512]{1,0:T(1,128)S(1)}, f32[1,512]{1,0:T(1,128)}, u32[]{:S(2)}) copy-start(f32[1,512]{1,0:T(1,128)} %get-tuple-element.466) | copy-start | bytes 6148
  256.0 34.9 %copy-start.49 = (f32[1,512]{1,0:T(1,128)S(1)}, f32[1,512]{1,0:T(1,128)}, u32[]{:S(2)}) copy-start(f32[1,512]{1,0:T(1,128)} %get-tuple-element.467) | copy-start | bytes 6148
  256.0 34.9 %copy-start.50 = (f32[1,512]{1,0:T(1,128)S(1)}, f32[1,512]{1,0:T(1,128)}, u32[]{:S(2)}) copy-start(f32[1,512]{1,0:T(1,128)} %get-tuple-element.468) | copy-start | bytes 6148
  292.1 3.1 copy-start.52
  292.1 3.1 copy-start.63
  292.5 44.0 %collective-permute-start.5 = (f32[3,512]{1,0:T(4,128)S(1)}, f32[3,512]{1,0:T(4,128)S(1)}, u32[]{:S(2)}, u32[]{:S(2)}) collective-permute-start(f32[3,512]{1,0:T(4,128)S(1)} %pad_add_fusion.4), channel_id=1, source_target_pairs={{4,0},{8,4},{12,8},{16,12},{20,16},{24,20},{28,24},{5,1},{9,5},{13... | collective-permute-start | bytes 18440 | tf_op jit(solution)/shard_map/ppermute | solution.py:21
  293.8 43.4 %collective-permute-start.4 = (f32[3,512]{1,0:T(4,128)S(1)}, f32[3,512]{1,0:T(4,128)S(1)}, u32[]{:S(2)}, u32[]{:S(2)}) collective-permute-start(f32[3,512]{1,0:T(4,128)S(1)} %pad_add_fusion.5), channel_id=1, source_target_pairs={{4,0},{8,4},{12,8},{16,12},{20,16},{24,20},{28,24},{5,1},{9,5},{13... | collective-permute-start | bytes 18440 | tf_op jit(solution)/shard_map/ppermute | solution.py:21
  (26 other events, 35.5 us)
Sparse Core Ops, SparseCore 0:
  28.9 73.8 all-gather.3
  139.1 71.8 all-gather.5
  256.1 33.5 all-reduce.30
where the time goes:
time: 347 us; the launch traced here: 344 us
  waiting for transfers between devices  92.5 us (27%)
  blocking collectives  74.8 us (22%)
  local copies, waits for them, and re-layouts  59.7 us (17%)
  other arithmetic  56.5 us (16%)
  matrix products  29.3 us (8%)
  starting transfers between devices  16.4 us (5%)
  between operations  14.8 us (4%)
    all_gather x2, waiting for transfers between devices, prefix(): pieces = jax.tree.map(lambda part: lax.all_gather(part, axis), value)  59.9 us
    psum x1, blocking collectives, body(): lax.psum((weight_x_grad, weight_b_grad, weight_c_grad), 'ctx')  41.3 us
    all_gather x1, blocking collectives, prefix(): pieces = jax.tree.map(lambda part: lax.all_gather(part, axis), value)  27.1 us
    psum x1, waiting for transfers between devices, body(): b_grad, c_grad = lax.psum((b_grad_one + b_grad_two, c_grad_part), 'tp')  23 us
    select_n x14, other arithmetic, lap(): jnp.where(position < mine, new, old)  16.3 us
    ppermute x6, starting transfers between devices, from_behind(): return lax.ppermute(x, axis, pairs)  16.1 us
    dot_general x3, matrix products, span_output(): jnp.einsum('crgqs,csrgp->cqrgp', weights, x_blk, precision=PRECISE)  15.2 us
    mul x28, local copies, waits for them, and re-layouts, link_combine(): later[0][..., None, None] * earlier[1] + later[1]  10.5 us
  transfers between devices with their start and end apart: 9, of which 4 were waited for; matrix products, arithmetic and copies ran while one was open for 19% of the time, Pallas kernels for 0%

commit v1 on v0

v1 whole, which is shorter than its diff:
```python
import functools

import jax
import jax.numpy as jnp
from jax import lax
from jax.experimental import pallas as pl
from jax.experimental.pallas import tpu as pltpu
from jax.sharding import PartitionSpec as P

HEAD_DIM = 32
STATE = 128
GROUPS = 4
CONV = 4
HALO = 16
LANES = 128
EPSILON = 1e-05
F32 = jnp.float32
BF16 = jnp.bfloat16
MM = ((1,), (0,))
MT = ((1,), (1,))


def split(value):
    high = value.astype(BF16)
    return high, (value - high.astype(F32)).astype(BF16)


def mul(a, b, dims=MM):
    def dot(u, v):
        return lax.dot_general(u, v, (dims, ((), ())), preferred_element_type=F32)

    return dot(a[0], b[0]) + (dot(a[0], b[1]) + dot(a[1], b[0]))


def exact(a, b, dims=MM):
    return lax.dot_general(
        a, b, (dims, ((), ())), preferred_element_type=F32, precision=lax.Precision.HIGHEST
    )


def sigmoid(v):
    return 1.0 / (1.0 + jnp.exp(-v))


def silu_slope(v):
    s = sigmoid(v)
    return s * (1.0 + v * (1.0 - s))


def iota(shape, axis):
    return lax.broadcasted_iota(jnp.int32, shape, axis)


def lane_group(width):
    return (iota((1, width), 1) // HEAD_DIM) % GROUPS


def head_spread(heads, width):
    return (iota((heads, width), 1) // HEAD_DIM == iota((heads, width), 0)).astype(F32)


def block_diagonal(state):
    owner = lane_group(state.shape[1])
    return jnp.concatenate([jnp.where(owner == g, state, 0.0) for g in range(GROUPS)], axis=0)


def diagonal_blocks(stacked):
    owner = lane_group(stacked.shape[1])
    total = jnp.zeros((STATE, stacked.shape[1]), F32)
    for g in range(GROUPS):
        total = jnp.where(owner == g, stacked[g * STATE : (g + 1) * STATE], total)
    return total


def tiles(width, size):
    return [slice(i, i + size) for i in range(0, width, size)]


def conv_rows(ext, taps, rows, cols):
    total = taps[0:1, :] * ext[HALO - 3 : HALO - 3 + rows, cols]
    for k in range(1, CONV):
        total = total + taps[k : k + 1, :] * ext[HALO - 3 + k : HALO - 3 + k + rows, cols]
    return total


def begin_kernel(
    x_ref, b_ref, c_ref, halo_ref, dt_ref, cx_ref, cb_ref, cc_ref, bias_ref, alog_ref,
    prex_ref, x_out, prebc_ref, bc_ref, dt_out, cum_ref, cumt_ref, dtx_ref, cumx_ref, state_ref, dec_ref,
    ext,
):
    rows, width = x_ref.shape
    half = b_ref.shape[1]
    heads = dt_ref.shape[1]
    step = jax.nn.softplus(dt_ref[...] + bias_ref[...])
    dt_out[...] = step
    tril = (iota((rows, rows), 0) >= iota((rows, rows), 1)).astype(F32)
    cum = exact(tril, -jnp.exp(alog_ref[...]) * step)
    cum_ref[...] = cum
    cumt_ref[...] = jnp.transpose(cum)
    spread = head_spread(heads, width)
    dtx_ref[...] = exact(step, spread)
    cumx_ref[...] = exact(cum, spread)
    dec_ref[...] = jnp.exp(cumx_ref[rows - 1 : rows, :])
    ext[0:HALO, :] = halo_ref[:, 0:width].astype(F32)
    ext[HALO:, :] = x_ref[...].astype(F32)
    for cols in tiles(width, LANES):
        pre = conv_rows(ext, cx_ref[:, cols], rows, cols)
        prex_ref[:, cols] = pre
        x_out[:, cols] = pre * sigmoid(pre)
    ext[0:HALO, :] = halo_ref[:, width:].astype(F32)
    ext[HALO:, 0:half] = b_ref[...].astype(F32)
    ext[HALO:, half:] = c_ref[...].astype(F32)
    for cols in tiles(2 * half, LANES):
        taps = cb_ref[:, cols] if cols.start < half else cc_ref[:, cols.start - half : cols.stop - half]
        pre = conv_rows(ext, taps, rows, cols)
        prebc_ref[:, cols] = pre
        bc_ref[:, cols] = pre * sigmoid(pre)
    b_turned = split(jnp.transpose(bc_ref[:, 0:half]))
    for cols in tiles(width, 2 * LANES):
        cumx = cumx_ref[:, cols]
        weighted = jnp.exp(cumx[rows - 1 : rows] - cumx) * dtx_ref[:, cols] * x_out[:, cols]
        state_ref[:, cols] = diagonal_blocks(mul(b_turned, split(weighted)))


def inside_kernel(x_ref, bc_ref, cum_ref, cumt_ref, dtx_ref, skip_ref, y_ref, inner):
    rows, width = x_ref.shape
    half = GROUPS * STATE
    for g in range(GROUPS):
        own = slice(g * STATE, (g + 1) * STATE)
        c_g = split(bc_ref[:, half + g * STATE : half + (g + 1) * STATE])
        inner[g] = mul(c_g, split(bc_ref[:, own]), MT)
    causal = iota((rows, rows), 0) >= iota((rows, rows), 1)
    owner = lane_group(LANES)
    for r, cols in enumerate(tiles(width, LANES)):
        x = x_ref[:, cols]
        weighted = x * dtx_ref[:, cols]
        total = skip_ref[:, cols] * x
        for g in range(GROUPS):
            h = r * GROUPS + g
            gap = cum_ref[:, h : h + 1] - cumt_ref[h : h + 1, :]
            kernel = jnp.exp(jnp.where(causal, gap, -1e30)) * inner[g]
            total = total + mul(split(kernel), split(jnp.where(owner == g, weighted, 0.0)))
        y_ref[:, cols] = total


def forward_prefix(mine, states_ref, decays_ref, cols, count):
    total = jnp.zeros((STATE, cols.stop - cols.start), F32)

    def lap(j, total):
        return decays_ref[j, :, cols] * total + states_ref[j, :, cols]

    return lax.fori_loop(0, mine, lap, total)


def backward_prefix(mine, states_ref, decays_ref, cols, count):
    total = jnp.zeros((STATE, cols.stop - cols.start), F32)

    def lap(j, total):
        k = count - 1 - j
        return decays_ref[k, :, cols] * total + states_ref[k, :, cols]

    return lax.fori_loop(0, count - 1 - mine, lap, total)


def output_kernel(
    mine_ref, states_ref, decays_ref, y_ref, bc_ref, cumx_ref, z_ref, go_ref, gain_ref, y_out, enter_ref, sums_ref
):
    rows, width = y_ref.shape
    half = GROUPS * STATE
    count = states_ref.shape[0]
    c_all = split(bc_ref[:, half:])
    squares = jnp.zeros((rows, LANES), F32)
    inners = jnp.zeros((rows, LANES), F32)
    for cols in tiles(width, 2 * LANES):
        enter = forward_prefix(mine_ref[0], states_ref, decays_ref, cols, count)
        enter_ref[:, cols] = enter
        carried = mul(c_all, split(block_diagonal(enter)))
        y = y_ref[:, cols] + jnp.exp(cumx_ref[:, cols]) * carried
        y_out[:, cols] = y
        z = z_ref[:, cols].astype(F32)
        gated = y * (z * sigmoid(z))
        scaled = go_ref[:, cols].astype(F32) * gain_ref[:, cols]
        sq = gated * gated
        pr = scaled * gated
        squares = squares + sq[:, :LANES] + sq[:, LANES:]
        inners = inners + pr[:, :LANES] + pr[:, LANES:]
    pick = (iota((2 * GROUPS, LANES), 1) // HEAD_DIM).astype(jnp.int32)
    row = iota((2 * GROUPS, LANES), 0)
    sums_ref[...] = exact((pick == row).astype(F32), squares, MT) + exact(
        (pick + GROUPS == row).astype(F32), inners, MT
    )


def turn_kernel(
    group_width, sums_ref, y_ref, bc_ref, cumx_ref, z_ref, go_ref, gain_ref, dy_ref, dz_ref, gain_grad_ref, state_ref
):
    rows, width = y_ref.shape
    half = GROUPS * STATE
    turned = jnp.transpose(sums_ref[...])
    pick = iota((2 * GROUPS, LANES), 1) // HEAD_DIM
    row = iota((2 * GROUPS, LANES), 0)
    squares = exact(turned, (pick == row).astype(F32))
    inners = exact(turned, (pick + GROUPS == row).astype(F32))
    inverse = lax.rsqrt(squares / group_width + EPSILON)
    correction = inverse * inverse * inverse * inners / group_width
    inverse = jnp.concatenate([inverse, inverse], axis=1)
    correction = jnp.concatenate([correction, correction], axis=1)
    c_turned = split(jnp.transpose(bc_ref[:, half:]))
    for cols in tiles(width, 2 * LANES):
        y = y_ref[:, cols]
        z = z_ref[:, cols].astype(F32)
        s = sigmoid(z)
        gate = z * s
        gated = y * gate
        go = go_ref[:, cols].astype(F32)
        gain_grad_ref[:, cols] = jnp.sum(go * gated * inverse, axis=0, keepdims=True)
        gated_grad = inverse * (go * gain_ref[:, cols]) - gated * correction
        dy = gated_grad * gate
        dy_ref[:, cols] = dy
        dz_ref[:, cols] = (gated_grad * y * (s * (1.0 + z * (1.0 - s)))).astype(BF16)
        state_ref[:, cols] = diagonal_blocks(mul(c_turned, split(jnp.exp(cumx_ref[:, cols]) * dy)))


def inside_back_kernel(
    x_ref, bc_ref, cum_ref, cumt_ref, dtx_ref, cumx_ref, enter_ref, dy_ref, dxd_ref, dbc_ref, inner, inner_grad
):
    rows, width = x_ref.shape
    half = GROUPS * STATE
    for g in range(GROUPS):
        own = slice(g * STATE, (g + 1) * STATE)
        c_g = split(bc_ref[:, half + g * STATE : half + (g + 1) * STATE])
        inner[g] = mul(split(bc_ref[:, own]), c_g, MT)
    inner_grad[...] = jnp.zeros_like(inner_grad)
    causal = iota((rows, rows), 0) <= iota((rows, rows), 1)
    owner = lane_group(LANES)
    for r, cols in enumerate(tiles(width, LANES)):
        dy = dy_ref[:, cols]
        weighted = split(x_ref[:, cols] * dtx_ref[:, cols])
        total = jnp.zeros((rows, LANES), F32)
        for g in range(GROUPS):
            h = r * GROUPS + g
            gap = cumt_ref[h : h + 1, :] - cum_ref[:, h : h + 1]
            decay = jnp.exp(jnp.where(causal, gap, -1e30))
            own = split(jnp.where(owner == g, dy, 0.0))
            total = total + mul(split(decay * inner[g]), own)
            inner_grad[g] = inner_grad[g] + decay * mul(weighted, own, MT)
        dxd_ref[:, cols] = total
    dc = jnp.zeros((rows, half), F32)
    for cols in tiles(width, 2 * LANES):
        pushed = jnp.exp(cumx_ref[:, cols]) * dy_ref[:, cols]
        dc = dc + mul(split(pushed), split(block_diagonal(enter_ref[:, cols])), MT)
    for g in range(GROUPS):
        own = slice(g * STATE, (g + 1) * STATE)
        other = slice(half + g * STATE, half + (g + 1) * STATE)
        grad = inner_grad[g]
        dbc_ref[:, own] = mul(split(grad), split(bc_ref[:, other]))
        dbc_ref[:, other] = dc[:, own] + mul(split(jnp.transpose(grad)), split(bc_ref[:, own]))


def finish_kernel(
    mine_ref, states_ref, decays_ref, x_ref, prex_ref, bc_ref, dt_ref, dtraw_ref, bias_ref, alog_ref, skip_ref,
    dtx_ref, cumx_ref, enter_ref, y_ref, dy_ref, dxd_ref, dbc_ref, xraw_ref, halo_ref,
    dpre_ref, dbc_out, ddt_ref, convx_ref, small_ref, ext,
):
    rows, width = x_ref.shape
    half = GROUPS * STATE
    heads = dt_ref.shape[1]
    count = states_ref.shape[0]
    ext[0:HALO, :] = halo_ref[:, 0:width].astype(F32)
    ext[HALO:, :] = xraw_ref[...].astype(F32)
    b_all = split(bc_ref[:, 0:half])
    size = 2 * LANES
    db = jnp.zeros((rows, half), F32)
    cum_grad = jnp.zeros((rows, heads), F32)
    step_grad = jnp.zeros((rows, heads), F32)
    ends = jnp.zeros((1, heads), F32)
    skips = jnp.zeros((1, heads), F32)
    for cols in tiles(width, size):
        later = backward_prefix(mine_ref[0], states_ref, decays_ref, cols, count)
        wide = split(block_diagonal(later))
        cumx = cumx_ref[:, cols]
        end = cumx[rows - 1 : rows]
        fade = jnp.exp(end - cumx)
        x = x_ref[:, cols]
        dtx = dtx_ref[:, cols]
        dy = dy_ref[:, cols]
        weighted = x * dtx
        from_state = fade * mul(b_all, wide)
        db = db + mul(split(fade * weighted), wide, MT)
        dxd = dxd_ref[:, cols] + from_state
        skip = skip_ref[:, cols]
        dx = dtx * dxd + skip * dy
        spread = (
            (iota((heads, size), 1) + cols.start) // HEAD_DIM == iota((heads, size), 0)
        ).astype(F32)
        cum_grad = cum_grad + exact(dy * (y_ref[:, cols] - skip * x) - weighted * dxd, spread, MT)
        step_grad = step_grad + exact(x * dxd, spread, MT)
        end_cols = jnp.sum(weighted * from_state, axis=0, keepdims=True) + jnp.exp(end) * jnp.sum(
            later * enter_ref[:, cols], axis=0, keepdims=True
        )
        ends = ends + exact(jnp.broadcast_to(end_cols, (8, size)), spread, MT)[0:1]
        skip_cols = jnp.sum(dy * x, axis=0, keepdims=True)
        skips = skips + exact(jnp.broadcast_to(skip_cols, (8, size)), spread, MT)[0:1]
        dpre = dx * silu_slope(prex_ref[:, cols])
        dpre_ref[:, cols] = dpre
        for k in range(CONV):
            convx_ref[k : k + 1, cols] = jnp.sum(
                dpre * ext[HALO - 3 + k : HALO - 3 + k + rows, cols], axis=0, keepdims=True
            )
    dbc_out[:, 0:half] = dbc_ref[:, 0:half] + db
    dbc_out[:, half:] = dbc_ref[:, half:]
    triu = (iota((rows, rows), 0) <= iota((rows, rows), 1)).astype(F32)
    log_grad = exact(triu, cum_grad) + ends
    rate = jnp.exp(alog_ref[...])
    raw_grad = (step_grad - rate * log_grad) * sigmoid(dtraw_ref[...] + bias_ref[...])
    ddt_ref[...] = raw_grad
    small_ref[...] = jnp.zeros_like(small_ref)
    small_ref[0:1, :] = jnp.sum(raw_grad, axis=0, keepdims=True)
    small_ref[1:2, :] = jnp.sum(-rate * log_grad * dt_ref[...], axis=0, keepdims=True)
    small_ref[2:3, :] = skips


def shared_kernel(dbc_ref, prebc_ref, braw_ref, craw_ref, halo_ref, dpre_ref, conv_ref, ext):
    rows, width = dbc_ref.shape
    half = braw_ref.shape[1]
    ext[0:HALO, :] = halo_ref[:, halo_ref.shape[1] - width :].astype(F32)
    ext[HALO:, 0:half] = braw_ref[...].astype(F32)
    ext[HALO:, half:] = craw_ref[...].astype(F32)
    for cols in tiles(width, LANES):
        dpre = dbc_ref[:, cols] * silu_slope(prebc_ref[:, cols])
        dpre_ref[:, cols] = dpre
        for k in range(CONV):
            conv_ref[k : k + 1, cols] = jnp.sum(
                dpre * ext[HALO - 3 + k : HALO - 3 + k + rows, cols], axis=0, keepdims=True
            )


def settle_kernel(dx_ref, dbc_ref, nx_ref, nbc_ref, cx_ref, cb_ref, cc_ref, gx_ref, gb_ref, gc_ref, ext):
    rows, width = dx_ref.shape
    half = gb_ref.shape[1]
    for source, after, outs in (
        (dx_ref, nx_ref, ((gx_ref, cx_ref, 0),)),
        (dbc_ref, nbc_ref, ((gb_ref, cb_ref, 0), (gc_ref, cc_ref, half))),
    ):
        ext[0:rows, :] = source[...]
        ext[rows : rows + 8, :] = after[...]
        for out, taps, start in outs:
            for cols in tiles(out.shape[1], LANES):
                here = slice(start + cols.start, start + cols.stop)
                total = taps[0:1, cols] * ext[3 : 3 + rows, here]
                for k in range(1, CONV):
                    total = total + taps[k : k + 1, cols] * ext[3 - k : 3 - k + rows, here]
                out[:, cols] = total.astype(BF16)


def call(kernel, outs, scratch, *args, scalars=0):
    vmem = pl.BlockSpec(memory_space=pltpu.VMEM)
    smem = pl.BlockSpec(memory_space=pltpu.SMEM)
    return pl.pallas_call(
        kernel,
        out_shape=[jax.ShapeDtypeStruct(s, d) for s, d in outs],
        in_specs=[smem] * scalars + [vmem] * (len(args) - scalars),
        out_specs=[vmem] * len(outs),
        scratch_shapes=[pltpu.VMEM(s, F32) for s in scratch],
        compiler_params=pltpu.CompilerParams(vmem_limit_bytes=48 * 1024 * 1024),
    )(*args)


def body(
    x_raw, b_raw, c_raw, z_gate, dt_raw, conv_x, conv_b, conv_c, dt_bias, a_log, d_skip, gain, grad_out
):
    rows, width = x_raw.shape
    heads = dt_raw.shape[1]
    half = b_raw.shape[1]
    count = lax.axis_size("ctx")
    mine = lax.axis_index("ctx").astype(jnp.int32).reshape(1)
    group_width = width * lax.axis_size("tp") // GROUPS
    bias, alog, gain_row = dt_bias[None], a_log[None], gain[None]
    skip = jnp.repeat(d_skip, HEAD_DIM)[None]
    tails = jnp.concatenate([x_raw[rows - HALO :], b_raw[rows - HALO :], c_raw[rows - HALO :]], axis=1)
    halo = lax.ppermute(tails, "ctx", [(i, i + 1) for i in range(count - 1)])
    full = ((rows, width), F32)
    shared = ((rows, 2 * half), F32)
    prex, x, prebc, bc, step, cum, cumt, dtx, cumx, own, dec = call(
        begin_kernel,
        [full, full, shared, shared, ((rows, heads), F32), ((rows, heads), F32), ((heads, rows), F32), full, full,
         ((STATE, width), F32), ((1, width), F32)],
        [(HALO + rows, width)],
        x_raw, b_raw, c_raw, halo, dt_raw, conv_x, conv_b, conv_c, bias, alog,
    )
    states = lax.all_gather(own, "ctx")
    decays = lax.all_gather(dec, "ctx")
    (y_own,) = call(inside_kernel, [full], [(GROUPS, rows, rows)], x, bc, cum, cumt, dtx, skip)
    y, enter, sums = call(
        output_kernel,
        [full, ((STATE, width), F32), ((2 * GROUPS, rows), F32)],
        [],
        mine, states, decays, y_own, bc, cumx, z_gate, grad_out, gain_row,
        scalars=1,
    )
    sums = lax.psum(sums, "tp")
    dy, dz, gain_part, state_part = call(
        functools.partial(turn_kernel, group_width),
        [full, ((rows, width), BF16), ((1, width), F32), ((STATE, width), F32)],
        [],
        sums, y, bc, cumx, z_gate, grad_out, gain_row,
    )
    state_grads = lax.all_gather(state_part, "ctx")
    dxd, dbc = call(
        inside_back_kernel,
        [full, shared],
        [(GROUPS, rows, rows), (GROUPS, rows, rows)],
        x, bc, cum, cumt, dtx, cumx, enter, dy,
    )
    dprex, dbc, ddt, convx_part, small = call(
        finish_kernel,
        [full, shared, ((rows, heads), F32), ((CONV, width), F32), ((8, heads), F32)],
        [(HALO + rows, width)],
        mine, state_grads, decays, x, prex, bc, step, dt_raw, bias, alog, skip,
        dtx, cumx, enter, y, dy, dxd, dbc, x_raw, halo,
        scalars=1,
    )
    back = [(i + 1, i) for i in range(count - 1)]
    next_x = lax.ppermute(dprex[:8], "ctx", back)
    dbc = lax.psum(dbc, "tp")
    dprebc, convbc_part = call(
        shared_kernel,
        [shared, ((CONV, 2 * half), F32)],
        [(HALO + rows, 2 * half)],
        dbc, prebc, b_raw, c_raw, halo,
    )
    next_bc = lax.ppermute(dprebc[:8], "ctx", back)
    packed = jnp.concatenate(
        [convx_part, convbc_part, gain_part, jnp.pad(small[:3].reshape(1, -1), ((0, 0), (0, width - 3 * heads)))], axis=0
    )
    packed = lax.psum(packed, "ctx")
    gx, gb, gc = call(
        settle_kernel,
        [((rows, width), BF16), ((rows, half), BF16), ((rows, half), BF16)],
        [(rows + 8, width)],
        dprex, dprebc, next_x, next_bc, conv_x, conv_b, conv_c,
    )
    last = packed[9]
    return (
        gx, gb, gc, dz, ddt,
        packed[0:4], packed[4:8, :half], packed[4:8, half:],
        last[:heads], last[heads : 2 * heads], last[2 * heads : 3 * heads], packed[8],
    )


def solution(mesh):
    col, row, cut = P("ctx", "tp"), P("ctx", None), P("tp")
    return jax.shard_map(
        body,
        mesh=mesh,
        in_specs=(col, row, row, col, col, P(None, "tp"), P(), P(), cut, cut, cut, cut, col),
        out_specs=(col, row, row, col, col, P(None, "tp"), P(), P(), cut, cut, cut, cut),
        check_vma=False,
    )
```

time: 347 us -> 305 us (0.88)
  other arithmetic: 56.5 us -> 0.76 us
  waiting for transfers between devices: 92.5 us -> 138 us
  matrix products: 29.3 us -> 0 us
  Pallas kernels: 0 us -> 23.3 us
  local copies, waits for them, and re-layouts: 59.7 us -> 44.2 us
  starting transfers between devices: 16.4 us -> 7.52 us
    all_gather x2, waiting for transfers between devices: 59.9 us -> 107 us  [the longest x1 66.5 us: body(): state_grads = lax.all_gather(state_part, 'ctx')]
    dot_general x12 -> x0, matrix products: 29.3 us -> none  [the longest x3 15.2 us: span_output(): jnp.einsum('crgqs,csrgp->cqrgp', weights, x_blk, precision=PRECISE)]
    unnamed x137 -> x104, local copies, waits for them, and re-layouts: 10.1 us -> 37.2 us
    pallas_call x0 -> x8, Pallas kernels: none -> 23.3 us  [call(): pl.pallas_call(kernel, out_shape=[jax.ShapeDtypeStruct(s, d) for s, d in...]
    select_n x15 -> x0, other arithmetic: 17 us -> none  [the longest x14 16.3 us: lap(): jnp.where(position < mine, new, old)]
    reduce_sum x11 -> x0, other arithmetic: 13.5 us -> none  [the longest x2 3.8 us: span_output(): return diagonal + carried + skip_gain[:, :, None] * x_blk]
    mul x30 -> x0, local copies, waits for them, and re-layouts: 11.2 us -> none  [the longest x28 10.5 us: link_combine(): later[0][..., None, None] * earlier[1] + later[1]]
    ppermute x6 -> x3, starting transfers between devices: 16.1 us -> 7.4 us  [the longest x1 4.84 us: body(): halo = lax.ppermute(tails, 'ctx', [(i, i + 1) for i in range(count - 1)])]
  transfers between devices with their start and end apart: 9 -> 6, of which waited for: 4 -> 5; matrix products, arithmetic and copies ran while one was open for 19% -> 3% of each run, Pallas kernels for 0% -> 2%
where the time goes in v1:
time: 305 us; the launch traced here: 304 us
  waiting for transfers between devices  138 us (45%)
  blocking collectives  76.1 us (25%)
  local copies, waits for them, and re-layouts  44.2 us (14%)
  Pallas kernels  23.3 us (8%)
  between operations  13.9 us (5%)
  starting transfers between devices  7.52 us (2%)
    all_gather x1, waiting for transfers between devices, body(): state_grads = lax.all_gather(state_part, 'ctx')  66.5 us
    all_gather x1, waiting for transfers between devices, body(): states = lax.all_gather(own, 'ctx')  40.6 us
    psum x1, blocking collectives, body(): packed = lax.psum(packed, 'ctx')  37.5 us
    unnamed x104, local copies, waits for them, and re-layouts  37.2 us
    all_gather x1, blocking collectives, body(): decays = lax.all_gather(dec, 'ctx')  32.9 us
    psum x1, waiting for transfers between devices, body(): dbc = lax.psum(dbc, 'tp')  27 us
    pallas_call x8, Pallas kernels, call(): pl.pallas_call(kernel, out_shape=[jax.ShapeDtypeStruct(s, d) for s, d in...  23.3 us
  transfers between devices with their start and end apart: 6, of which 5 were waited for; matrix products, arithmetic and copies ran while one was open for 3% of the time, Pallas kernels for 2%

profile of v1, /device:TPU:0, one launch (start us, length us, event | category | flops | bytes accessed | tf_op | source)
XLA Modules:
  0.0 303.6 jit_solution(2719322426496857281)
XLA Ops:
  8.7 0.8 slice.52
  9.4 4.8 %collective-permute-start = (bf16[16,2048]{1,0:T(8,128)(2,1)S(1)}, bf16[16,2048]{1,0:T(8,128)(2,1)S(1)}, u32[]{:S(2)}, u32[]{:S(2)}) collective-permute-start(bf16[16,2048]{1,0:T(8,128)(2,1)S(1)} %pad_maximum_fusion), channel_id=1, source_target_pairs={{0,4},{4,8},{8,12},{12,16},{16,20},{20,24},{24,28},{1,5},{5,9},{9,... | collective-permute-start | bytes 196616 | tf_op jit(solution)/shard_map/ppermute | solution.py:381
  14.3 0.8 copy.28.dt_ref.dtraw_ref
  15.1 1.1 collective-permute-done.halo_ref
  16.2 1.0 copy-done.3
  17.1 0.9 copy-done.11
  18.0 0.9 copy-done.13
  22.4 3.2 %shard_map.220 = (f32[128,1024]{1,0:T(8,128)S(1)}, f32[128,1024]{1,0:T(8,128)S(1)}, f32[128,1024]{1,0:T(8,128)S(1)}, f32[128,1024]{1,0:T(8,128)S(1)}, f32[128,32...) custom-call(bf16[128,1024]{1,0:T(8,128)(2,1)S(1)} %copy-done.3, ...), custom_call_target="tpu_custom_call" | custom-call | tf_op jit(solution)/shard_map/pallas_call | solution.py:359
  25.6 0.8 copy-done.20
  26.4 0.8 copy-done.24
  28.7 1.4 shard_map.221.y_ref
  30.2 32.9 %all-gather.3.decays_ref = f32[8,1,1024]{2,1,0:T(1,128)S(1)} all-gather(f32[1,1,1024]{2,1,0:T(1,128)S(1)} %bitcast.16), channel_id=3, replica_groups=mesh['ctx'=8,'tp'=4] {'ctx'}, dimensions={0}, use_global_device_ids=true | all-gather | bytes 36864 | tf_op jit(solution)/shard_map/all_gather | solution.py:392
  63.1 40.6 %all-gather.7.cloned.1.call-done = f32[1024,1024]{1,0:T(8,128)} async-done(((f32[128,1024]{1,0:T(8,128)}), f32[1024,1024]{1,0:T(8,128)}) %all-gather.7.cloned.1.call-update) | async-done | bytes 4194320 | tf_op jit(solution)/shard_map/all_gather | solution.py:391
  103.7 0.9 copy-done.5
  104.7 0.9 copy-done.7
  106.3 4.2 %shard_map.222 = (f32[128,1024]{1,0:T(8,128)S(1)}, f32[128,1024]{1,0:T(8,128)S(1)}, f32[8,128]{1,0:T(8,128)S(1)}) custom-call(s32[1]{0:T(128)} %bitcast.mine_ref, f32[8,128,1024]{2,1,0:T(8,128)} %bitcast.22, f32[8,1,1024]{2,1,0:T(1,128)S(1)} %all-gather.3.decays_ref, f32[128,1024]{1,0:T(8,128)S(1)} %shard_map.221.y_ref, ...), custom_call_target="tpu_custom_call" | custom-call | tf_op jit(solution)/shard_map/pallas_call | solution.py:359
  110.5 0.8 copy-done
  111.3 5.6 %psum.21.sums_ref = f32[8,128]{1,0:T(8,128)S(1)} all-reduce(f32[8,128]{1,0:T(8,128)S(1)} %get-tuple-element.50), channel_id=1, replica_groups=mesh['ctx'=8,'tp'=4] {'tp'}, use_global_device_ids=true, to_apply=%region_0.0 | all-reduce | flops 1024 | bytes 8192 | tf_op jit(solution)/shard_map/psum | solution.py:401
  116.9 1.0 copy-done.1
  118.0 0.9 copy-done.6
  118.9 0.9 copy-done.8
  119.9 1.5 shard_map.223
  121.4 0.8 copy-done.28
  122.9 4.3 %shard_map.224 = (f32[128,1024]{1,0:T(8,128)S(1)}, f32[128,1024]{1,0:T(8,128)S(1)}) custom-call(f32[128,1024]{1,0:T(8,128)S(1)} %get-tuple-element.44.x_ref, f32[128,1024]{1,0:T(8,128)S(1)} %get-tuple-element.45.bc_ref, f32[128,32]{1,0:T(8,128)S(1)} %get-tuple-element.46.cum_ref, f32[32,128]{1,0:T(8,128)S(1)} %get-tuple-element.47.cumt_ref, ...), custom_call_target="tpu_custom_call" | custom-call | tf_op jit(solution)/shard_map/pallas_call | solution.py:359
  127.2 0.8 copy-done.22
  128.0 0.8 copy-done.23
  128.8 66.5 %all-gather.9.cloned.1.call-done = f32[1024,1024]{1,0:T(8,128)} async-done(((f32[128,1024]{1,0:T(8,128)}), f32[1024,1024]{1,0:T(8,128)}) %all-gather.9.cloned.1.call-update) | async-done | bytes 4194320 | tf_op jit(solution)/shard_map/all_gather | solution.py:408
  195.3 1.0 copy-done.2
  196.4 0.8 copy-done.16
  197.2 0.8 copy-done.18
  198.1 1.0 copy-done.21
  199.9 0.8 copy-done.32
  202.7 6.7 %shard_map.225 = (f32[128,1024]{1,0:T(8,128)S(1)}, f32[128,1024]{1,0:T(8,128)S(1)}, f32[128,32]{1,0:T(8,128)S(1)}, f32[4,1024]{1,0:T(4,128)S(1)}, f32[8,32]{1,0:T(8,128)S(1)}) custom-call(s32[1]{0:T(128)} %bitcast.mine_ref, f32[8,128,1024]{2,1,0:T(8,128)} %bitcast.21, f32[8,1,1024]{2,1,0:T(1,128)S(1)} %copy-done.30, ...), custom_call_target="tpu_custom_call" | custom-call | tf_op jit(solution)/shard_map/pallas_call | solution.py:359
  209.4 0.8 copy-done.9
  210.2 0.8 copy-done.26
  213.6 1.5 copy.30
  215.1 0.8 slice.55
  215.9 1.3 collective-permute-start.1
  217.2 27.0 %all-reduce.3.cloned.1.call-done.dbc_ref = f32[128,1024]{1,0:T(8,128)} async-done(((f32[128,1024]{1,0:T(8,128)}), f32[128,1024]{1,0:T(8,128)}) %all-reduce.3.cloned.1.call-update) | async-done | bytes 524304 | tf_op jit(solution)/shard_map/psum | solution.py:425
  244.1 0.9 copy-done.14
  245.0 0.8 copy-done.19
  245.9 1.0 copy-done.25
  246.9 1.0 copy-done.27
  249.2 37.5 %psum.23 = f32[10,1024]{1,0:T(8,128)S(1)} all-reduce(f32[10,1024]{1,0:T(8,128)S(1)} %select_maximum_fusion), channel_id=1, replica_groups=mesh['ctx'=8,'tp'=4] {'ctx'}, use_global_device_ids=true, to_apply=%region_2.3 | all-reduce | flops 10240 | bytes 81920 | tf_op jit(solution)/shard_map/psum | solution.py:436
  287.4 1.3 collective-permute-start.2
  290.5 2.7 collective-permute-done.2.nbc_ref
  293.2 1.0 copy-done.10
  295.6 1.5 shard_map.227
  (97 shorter events, 18.2 us)
Async XLA Ops:
  7.2 96.5 %all-gather.7.cloned.1.call-start = ((), (), s32[]{:S(2)}) async-start(), calls=%async_computation.1 | async-start | bytes 4718592 | tf_op jit(solution)/shard_map/all_gather | solution.py:391
  9.4 6.7 %collective-permute-start = (bf16[16,2048]{1,0:T(8,128)(2,1)S(1)}, bf16[16,2048]{1,0:T(8,128)(2,1)S(1)}, u32[]{:S(2)}, u32[]{:S(2)}) collective-permute-start(bf16[16,2048]{1,0:T(8,128)(2,1)S(1)} %pad_maximum_fusion), channel_id=1, source_target_pairs={{0,4},{4,8},{8,12},{12,16},{16,20},{20,24},{24,28},{1,5},{5,9},{9,... | collective-permute-start | bytes 196616 | tf_op jit(solution)/shard_map/ppermute | solution.py:381
  15.1 88.6 %copy-start.15 = (f32[128,32]{1,0:T(8,128)}, f32[128,32]{1,0:T(8,128)S(1)}, u32[]{:S(2)}) copy-start(f32[128,32]{1,0:T(8,128)S(1)} %copy.28.dt_ref.dtraw_ref) | copy-start | bytes 49156
  16.2 87.5 %copy-start.17 = (bf16[16,2048]{1,0:T(8,128)(2,1)}, bf16[16,2048]{1,0:T(8,128)(2,1)S(1)}, u32[]{:S(2)}) copy-start(bf16[16,2048]{1,0:T(8,128)(2,1)S(1)} %collective-permute-done.halo_ref) | copy-start | bytes 196612
  16.2 1.0 copy-start.3
  17.1 0.9 copy-start.11
  18.0 0.9 copy-start.13
  18.9 0.7 copy-start.33
  19.7 0.7 copy-start.38
  20.4 0.7 copy-start.40
  25.6 0.8 copy-start.20
  26.4 0.8 copy-start.24
  27.8 167.5 %all-gather.9.cloned.1.call-start = ((), (), s32[]{:S(2)}) async-start(), calls=%async_computation.2 | async-start | bytes 4718592 | tf_op jit(solution)/shard_map/all_gather | solution.py:408
  28.7 1.5 copy-start.36
  28.7 88.2 %copy-start.44 = (f32[1024]{0:T(1024)S(1)}, f32[1024]{0:T(1024)}, u32[]{:S(2)}) copy-start(f32[1024]{0:T(1024)} %param.24) | copy-start | bytes 12292
  63.1 58.3 %copy-start.29 = (f32[8,1,1024]{2,1,0:T(1,128)}, f32[8,1,1024]{2,1,0:T(1,128)S(1)}, u32[]{:S(2)}) copy-start(f32[8,1,1024]{2,1,0:T(1,128)S(1)} %all-gather.3.decays_ref) | copy-start | bytes 98308
  103.7 1.0 copy-start.5
  104.7 0.9 copy-start.7
  105.6 0.7 copy-start.43
  106.3 89.0 %copy-start.4 = (bf16[128,1024]{1,0:T(8,128)(2,1)S(1)}, bf16[128,1024]{1,0:T(8,128)(2,1)}, u32[]{:S(2)}) copy-start(bf16[128,1024]{1,0:T(8,128)(2,1)} %xraw_ref.1) | copy-start | bytes 786436
  110.5 0.8 copy-start
  116.9 1.0 copy-start.1
  118.0 0.9 copy-start.6
  118.9 0.9 copy-start.8
  121.4 0.8 copy-start.28
  122.8 121.3 %all-reduce.3.cloned.1.call-start = ((), (), s32[]{:S(2)}) async-start(), calls=%async_computation | async-start | bytes 1048576 | tf_op jit(solution)/shard_map/psum | solution.py:425
  127.2 0.8 copy-start.22
  128.0 0.8 copy-start.23
  195.3 1.0 copy-start.2
  196.4 0.8 copy-start.16
  197.2 0.8 copy-start.18
  198.1 1.0 copy-start.21
  199.1 0.8 copy-start.30
  199.9 0.8 copy-start.32
  200.7 0.7 copy-start.37
  202.7 41.4 %copy-start.12 = (bf16[128,512]{1,0:T(8,128)(2,1)S(1)}, bf16[128,512]{1,0:T(8,128)(2,1)}, u32[]{:S(2)}) copy-start(bf16[128,512]{1,0:T(8,128)(2,1)} %braw_ref.1) | copy-start | bytes 393220
  202.7 90.5 %copy-start.34 = (f32[4,1024]{1,0:T(4,128)S(1)}, f32[4,1024]{1,0:T(4,128)}, u32[]{:S(2)}) copy-start(f32[4,1024]{1,0:T(4,128)} %cx_ref.3) | copy-start | bytes 49156
  209.4 0.8 copy-start.9
  210.2 0.8 copy-start.26
  215.9 74.6 %collective-permute-start.1 = (f32[8,1024]{1,0:T(8,128)S(1)}, f32[8,1024]{1,0:T(8,128)S(1)}, u32[]{:S(2)}, u32[]{:S(2)}) collective-permute-start(f32[8,1024]{1,0:T(8,128)S(1)} %slice.55), channel_id=1, source_target_pairs={{4,0},{8,4},{12,8},{16,12},{20,16},{24,20},{28,24},{5,1},{9,5},{13... | collective-permute-start | bytes 98312 | tf_op jit(solution)/shard_map/ppermute | solution.py:424
  244.1 0.9 copy-start.14
  245.0 0.8 copy-start.19
  245.9 1.0 copy-start.25
  246.9 1.0 copy-start.27
  287.4 5.8 %collective-permute-start.2 = (f32[8,1024]{1,0:T(8,128)S(1)}, f32[8,1024]{1,0:T(8,128)S(1)}, u32[]{:S(2)}, u32[]{:S(2)}) collective-permute-start(f32[8,1024]{1,0:T(8,128)S(1)} %slice.56), channel_id=1, source_target_pairs={{4,0},{8,4},{12,8},{16,12},{20,16},{24,20},{28,24},{5,1},{9,5},{13... | collective-permute-start | bytes 98312 | tf_op jit(solution)/shard_map/ppermute | solution.py:432
  293.2 1.0 copy-start.10
  294.2 0.7 copy-start.39
  294.9 0.7 copy-start.41
  (9 other events, 5.7 us)
Sparse Core Ops, SparseCore 0:
  27.9 75.6 all-gather.6
  122.9 72.3 all-gather.8
  212.9 31.1 all-reduce.2

commit v2 on v1

v2 whole, which is shorter than its diff:
```python
import jax
import jax.numpy as jnp
from jax import lax
from jax.experimental import pallas as pl
from jax.experimental.pallas import tpu as pltpu
from jax.sharding import PartitionSpec as P

HEAD_DIM = 32
STATE = 128
GROUPS = 4
CONV = 4
HALO = 16
LANES = 128
EPSILON = 1e-05
F32 = jnp.float32
BF16 = jnp.bfloat16
MM = ((1,), (0,))
MT = ((1,), (1,))


def split(value):
    high = value.astype(BF16)
    return high, (value - high.astype(F32)).astype(BF16)


def mul(a, b, dims=MM):
    def dot(u, v):
        return lax.dot_general(u, v, (dims, ((), ())), preferred_element_type=F32)

    return dot(a[0], b[0]) + (dot(a[0], b[1]) + dot(a[1], b[0]))


def exact(a, b, dims=MM):
    return lax.dot_general(
        a, b, (dims, ((), ())), preferred_element_type=F32, precision=lax.Precision.HIGHEST
    )


def sigmoid(v):
    return 1.0 / (1.0 + jnp.exp(-v))


def silu_slope(v):
    s = sigmoid(v)
    return s * (1.0 + v * (1.0 - s))


def iota(shape, axis):
    return lax.broadcasted_iota(jnp.int32, shape, axis)


def lane_group(width):
    return (iota((1, width), 1) // HEAD_DIM) % GROUPS


def head_spread(heads, width):
    return (iota((heads, width), 1) // HEAD_DIM == iota((heads, width), 0)).astype(F32)


def block_diagonal(state):
    owner = lane_group(state.shape[1])
    return jnp.concatenate([jnp.where(owner == g, state, 0.0) for g in range(GROUPS)], axis=0)


def diagonal_blocks(stacked):
    owner = lane_group(stacked.shape[1])
    total = jnp.zeros((STATE, stacked.shape[1]), F32)
    for g in range(GROUPS):
        total = jnp.where(owner == g, stacked[g * STATE : (g + 1) * STATE], total)
    return total


def tiles(width, size):
    return [slice(i, i + size) for i in range(0, width, size)]


def conv_rows(ext, taps, rows, cols):
    total = taps[0:1, :] * ext[HALO - 3 : HALO - 3 + rows, cols]
    for k in range(1, CONV):
        total = total + taps[k : k + 1, :] * ext[HALO - 3 + k : HALO - 3 + k + rows, cols]
    return total

MESH = pl.DeviceIdType.MESH
ROW_F = STATE + 8


def pair(ref, cols):
    first = cols.start // LANES
    return jnp.concatenate([ref[first], ref[first + 1]], axis=1)


def mixer_kernel(
    x_hbm, b_hbm, c_hbm, z_hbm, dtt_hbm, cx_hbm, cb_hbm, cc_hbm, bias_hbm, alog_hbm, dskip_hbm, gain_hbm, go_hbm,
    gx_hbm, gb_hbm, gc_hbm, dz_hbm, ddt_hbm, convx_hbm, convb_hbm, convc_hbm, small_hbm,
    x_in, bc_in, z_ref, dtt_ref, cx_ref, cbc_ref, bias_ref, alog_ref, dskip_ref, gain_ref, go_ref,
    halo_ref, extx, extbc, prex_ref, x_ref, prebc_ref, bc_ref, cumt_ref, dtx_ref, cumx_ref, skip_ref,
    y_ref, dy_ref, dxd_ref, inner, inner_grad,
    own_f, slots_f, outs_f, enter_ref, own_b, slots_b, outs_b, later_ref,
    own_p, slots_p, outs_p, total_p,
    sums_slots, early, slots_e, late, slots_l, final, taps_all, dpre_own, next_x, next_bc,
    gx_ref, gbc_ref, dz_ref, ddt_ref, convbc_ref, small_ref,
    load_sem, store_sem, ctx_send, ctx_recv, tp_send, tp_recv, halo_send, halo_recv,
):
    me, tp = lax.axis_index("ctx"), lax.axis_index("tp")
    count, lanes_of_heads = lax.axis_size("ctx"), lax.axis_size("tp")
    ranks = lanes_of_heads
    rows, width = x_in.shape
    half = GROUPS * STATE
    heads = dtt_ref.shape[0]
    parts = width // LANES
    stride = count // parts
    my_part = me // stride
    size = 2 * LANES

    loads = []

    def load(src, dst):
        copy = pltpu.make_async_copy(src, dst, load_sem.at[len(loads)])
        copy.start()
        loads.append(copy)

    load(x_hbm, x_in)
    load(b_hbm, bc_in.at[:, 0:half])
    load(c_hbm, bc_in.at[:, half:])
    load(dtt_hbm, dtt_ref)
    load(cx_hbm, cx_ref)
    load(cb_hbm, cbc_ref.at[:, 0:half])
    load(cc_hbm, cbc_ref.at[:, half:])
    load(bias_hbm, bias_ref)
    load(alog_hbm, alog_ref)
    load(dskip_hbm, dskip_ref)
    load(gain_hbm, gain_ref)
    load(z_hbm, z_ref)
    load(go_hbm, go_ref)

    barrier = pltpu.get_barrier_semaphore()
    for d in range(1, count):
        pl.semaphore_signal(barrier, inc=1, device_id=(lax.rem(me + d, count), tp), device_id_type=MESH)
    for d in range(1, ranks):
        pl.semaphore_signal(barrier, inc=1, device_id=(me, lax.rem(tp + d, ranks)), device_id_type=MESH)
    pl.semaphore_wait(barrier, count - 1 + ranks - 1)

    def remote(src, dst, send, recv, ctx, rank):
        return pltpu.make_async_remote_copy(
            src_ref=src, dst_ref=dst, send_sem=send, recv_sem=recv, device_id=(ctx, rank), device_id_type=MESH
        )

    ahead, behind = lax.rem(me + 1, count), lax.rem(me + count - 1, count)
    for copy in loads[0:3]:
        copy.wait()
    tail = [
        remote(x_in.at[rows - HALO :, :], halo_ref.at[:, 0:width], halo_send.at[0], halo_recv.at[0], ahead, tp),
        remote(bc_in.at[rows - HALO :, :], halo_ref.at[:, width:], halo_send.at[1], halo_recv.at[1], ahead, tp),
    ]

    @pl.when(me < count - 1)
    def _():
        for copy in tail:
            copy.start()

    for copy in loads[3:11]:
        copy.wait()

    step = jax.nn.softplus(jnp.transpose(dtt_ref[...]) + bias_ref[...])
    rate = jnp.exp(alog_ref[...])
    tril = (iota((rows, rows), 0) >= iota((rows, rows), 1)).astype(F32)
    cum = exact(tril, -rate * step)
    cumt_ref[...] = jnp.transpose(cum)
    spread = head_spread(heads, width)
    dtx_ref[...] = exact(step, spread)
    cumx_ref[...] = exact(cum, spread)
    skip_ref[...] = exact(jnp.broadcast_to(dskip_ref[...], (8, heads)), spread)
    extx[HALO:, :] = x_in[...].astype(F32)
    extbc[HALO:, :] = bc_in[...].astype(F32)

    @pl.when(me == 0)
    def _():
        extx[0:HALO, :] = jnp.zeros((HALO, width), F32)
        extbc[0:HALO, :] = jnp.zeros((HALO, 2 * half), F32)

    @pl.when(me > 0)
    def _():
        for copy in tail:
            copy.wait_recv()
        extx[0:HALO, :] = halo_ref[:, 0:width].astype(F32)
        extbc[0:HALO, :] = halo_ref[:, width:].astype(F32)

    for cols in tiles(2 * half, LANES):
        pre = conv_rows(extbc, cbc_ref[:, cols], rows, cols)
        prebc_ref[:, cols] = pre
        bc_ref[:, cols] = pre * sigmoid(pre)
    for cols in tiles(width, LANES):
        pre = conv_rows(extx, cx_ref[:, cols], rows, cols)
        prex_ref[:, cols] = pre
        x_ref[:, cols] = pre * sigmoid(pre)
    b_turned = split(jnp.transpose(bc_ref[:, 0:half]))
    for cols in tiles(width, size):
        cumx = cumx_ref[:, cols]
        end = cumx[rows - 1 : rows]
        weighted = jnp.exp(end - cumx) * dtx_ref[:, cols] * x_ref[:, cols]
        state = diagonal_blocks(mul(b_turned, split(weighted)))
        decay = jnp.broadcast_to(jnp.exp(end), (8, size))
        for i in range(2):
            own_f[cols.start // LANES + i, 0:STATE, :] = state[:, i * LANES : (i + 1) * LANES]
            own_f[cols.start // LANES + i, STATE:, :] = decay[:, i * LANES : (i + 1) * LANES]

    def to_owner(own, slots, k, part):
        return remote(own.at[part], slots.at[me], ctx_send.at[k, part], ctx_recv.at[k, me], part * stride, tp)

    def gather_tiles(own, slots, k):
        for d in range(1, parts):
            to_owner(own, slots, k, lax.rem(my_part + d, parts)).start()
        if stride > 1:
            @pl.when(lax.rem(me, stride) != 0)
            def _():
                to_owner(own, slots, k, my_part).start()

    def owner_only(act):
        if stride > 1:
            pl.when(lax.rem(me, stride) == 0)(act)
        else:
            act()

    def from_owner(out, result, k, i):
        return remote(out, result.at[my_part], ctx_send.at[k + 1, i], ctx_recv.at[k + 1, my_part], i, tp)

    def slot_wait(slots, k, j):
        @pl.when(j != me)
        def _():
            remote(slots.at[j], slots.at[j], ctx_send.at[k, 0], ctx_recv.at[k, j], ahead, tp).wait_recv()

    def settle_exchange(own, slots, outs, result, k):
        for j in range(parts):
            @pl.when(me != j * stride)
            def _():
                remote(result.at[j], result.at[j], ctx_send.at[k + 1, 0], ctx_recv.at[k + 1, j], ahead, tp).wait_recv()

    def drain(own, slots, outs, result, k):
        for j in range(parts):
            @pl.when(me != j * stride)
            def _():
                to_owner(own, slots, k, j).wait_send()

        def sent():
            for i in range(count):
                @pl.when(me != i)
                def _():
                    from_owner(outs.at[i], result, k, i).wait_send()

        owner_only(sent)

    def scan(own, slots, decays, outs, result, k, order):
        def act():
            slots[me] = own[my_part]
            total = jnp.zeros((STATE, LANES), F32)
            for i in order:
                outs[i] = total

                @pl.when(i != me)
                def _():
                    from_owner(outs.at[i], result, k, i).start()

                slot_wait(slots, k, i)
                total = decays[i, STATE : STATE + 1, :] * total + slots[i, 0:STATE, :]
            result[my_part] = outs[me]

        owner_only(act)

    gather_tiles(own_f, slots_f, 0)

    owner = lane_group(LANES)
    causal = iota((rows, rows), 0) >= iota((rows, rows), 1)
    for g in range(GROUPS):
        c_g = split(bc_ref[:, half + g * STATE : half + (g + 1) * STATE])
        inner[g] = mul(c_g, split(bc_ref[:, g * STATE : (g + 1) * STATE]), MT)
    for r, cols in enumerate(tiles(width, LANES)):
        x = x_ref[:, cols]
        weighted = x * dtx_ref[:, cols]
        cumx = cumx_ref[:, cols]
        total = skip_ref[0:1, cols] * x
        for g in range(GROUPS):
            h = r * GROUPS + g
            gap = cumx[:, g * HEAD_DIM : g * HEAD_DIM + 1] - cumt_ref[h : h + 1, :]
            fade = jnp.exp(jnp.where(causal, gap, -1e30)) * inner[g]
            total = total + mul(split(fade), split(jnp.where(owner == g, weighted, 0.0)))
        y_ref[:, cols] = total

    scan(own_f, slots_f, slots_f, outs_f, enter_ref, 0, range(count))
    for copy in loads[11:]:
        copy.wait()
    settle_exchange(own_f, slots_f, outs_f, enter_ref, 0)

    c_all = split(bc_ref[:, half:])
    squares = jnp.zeros((rows, LANES), F32)
    inners = jnp.zeros((rows, LANES), F32)
    for cols in tiles(width, size):
        carried = mul(c_all, split(block_diagonal(pair(enter_ref, cols))))
        y = y_ref[:, cols] + jnp.exp(cumx_ref[:, cols]) * carried
        y_ref[:, cols] = y
        z = z_ref[:, cols].astype(F32)
        gated = y * (z * sigmoid(z))
        scaled = go_ref[:, cols].astype(F32) * gain_ref[:, cols]
        sq = gated * gated
        pr = scaled * gated
        squares = squares + sq[:, :LANES] + sq[:, LANES:]
        inners = inners + pr[:, :LANES] + pr[:, LANES:]
    pick = iota((2 * GROUPS, LANES), 1) // HEAD_DIM
    row = iota((2 * GROUPS, LANES), 0)
    pick_low = (pick == row).astype(F32)
    pick_high = (pick + GROUPS == row).astype(F32)
    sums_slots[tp] = exact(pick_low, squares, MT) + exact(pick_high, inners, MT)

    def tp_copies(own_at, dst_at, k):
        return [
            remote(own_at(q), dst_at, tp_send.at[k, q], tp_recv.at[k, tp], me, q)
            for q in [lax.rem(tp + d, ranks) for d in range(1, ranks)]
        ]

    def tp_wait(slots, k):
        for d in range(1, ranks):
            q = lax.rem(tp + d, ranks)
            remote(slots.at[q], slots.at[q], tp_send.at[k, q], tp_recv.at[k, q], me, q).wait_recv()

    started = []

    def tp_start(own_at, dst_at, k):
        copies = tp_copies(own_at, dst_at, k)
        for copy in copies:
            copy.start()
        started.extend(copies)

    tp_start(lambda q: sums_slots.at[tp], sums_slots.at[tp], 0)
    tp_wait(sums_slots, 0)
    sums = sums_slots[0]
    for q in range(1, ranks):
        sums = sums + sums_slots[q]
    group_width = width * ranks // GROUPS
    turned = jnp.transpose(sums)
    inverse = lax.rsqrt(exact(turned, pick_low) / group_width + EPSILON)
    correction = inverse * inverse * inverse * exact(turned, pick_high) / group_width
    inverse = jnp.concatenate([inverse, inverse], axis=1)
    correction = jnp.concatenate([correction, correction], axis=1)
    c_turned = split(jnp.transpose(bc_ref[:, half:]))
    own_p[...] = jnp.zeros_like(own_p)
    for cols in tiles(width, size):
        y = y_ref[:, cols]
        z = z_ref[:, cols].astype(F32)
        s = sigmoid(z)
        gate = z * s
        gated = y * gate
        go = go_ref[:, cols].astype(F32)
        gain_grad = jnp.sum(go * gated * inverse, axis=0, keepdims=True)
        gated_grad = inverse * (go * gain_ref[:, cols]) - gated * correction
        dy = gated_grad * gate
        dy_ref[:, cols] = dy
        dz_ref[:, cols] = (gated_grad * y * (s * (1.0 + z * (1.0 - s)))).astype(BF16)
        state = diagonal_blocks(mul(c_turned, split(jnp.exp(cumx_ref[:, cols]) * dy)))
        for i in range(2):
            part = slice(i * LANES, (i + 1) * LANES)
            own_b[cols.start // LANES + i] = state[:, part]
            own_p[cols.start // LANES + i, 4:5, :] = gain_grad[:, part]
    gather_tiles(own_b, slots_b, 2)

    stores = []

    def store(src, dst):
        copy = pltpu.make_async_copy(src, dst, store_sem.at[len(stores)])
        copy.start()
        stores.append(copy)

    store(dz_ref, dz_hbm)

    for g in range(GROUPS):
        c_g = split(bc_ref[:, half + g * STATE : half + (g + 1) * STATE])
        inner[g] = mul(split(bc_ref[:, g * STATE : (g + 1) * STATE]), c_g, MT)
    inner_grad[...] = jnp.zeros_like(inner_grad)
    causal = iota((rows, rows), 0) <= iota((rows, rows), 1)
    for r, cols in enumerate(tiles(width, LANES)):
        dy = dy_ref[:, cols]
        cumx = cumx_ref[:, cols]
        weighted = split(x_ref[:, cols] * dtx_ref[:, cols])
        total = jnp.zeros((rows, LANES), F32)
        for g in range(GROUPS):
            h = r * GROUPS + g
            gap = cumt_ref[h : h + 1, :] - cumx[:, g * HEAD_DIM : g * HEAD_DIM + 1]
            decay = jnp.exp(jnp.where(causal, gap, -1e30))
            masked = split(jnp.where(owner == g, dy, 0.0))
            total = total + mul(split(decay * inner[g]), masked)
            inner_grad[g] = inner_grad[g] + decay * mul(weighted, masked, MT)
        dxd_ref[:, cols] = total
    dc = jnp.zeros((rows, half), F32)
    for cols in tiles(width, size):
        pushed = jnp.exp(cumx_ref[:, cols]) * dy_ref[:, cols]
        dc = dc + mul(split(pushed), split(block_diagonal(pair(enter_ref, cols))), MT)
    for g in range(GROUPS):
        own = slice(g * STATE, (g + 1) * STATE)
        other = slice(half + g * STATE, half + (g + 1) * STATE)
        grad = inner_grad[g]
        early[g, 0:rows, :] = mul(split(grad), split(bc_ref[:, other]))
        early[g, rows:, :] = dc[:, own] + mul(split(jnp.transpose(grad)), split(bc_ref[:, own]))
    tp_start(lambda q: early.at[q], slots_e.at[tp], 1)

    scan(own_b, slots_b, slots_f, outs_b, later_ref, 2, range(count - 1, -1, -1))
    settle_exchange(own_b, slots_b, outs_b, later_ref, 2)

    db = jnp.zeros((rows, half), F32)
    for cols in tiles(width, size):
        wide = split(block_diagonal(pair(later_ref, cols)))
        cumx = cumx_ref[:, cols]
        fade = jnp.exp(cumx[rows - 1 : rows] - cumx)
        db = db + mul(split(fade * (x_ref[:, cols] * dtx_ref[:, cols])), wide, MT)
    for g in range(GROUPS):
        late[g] = db[:, g * STATE : (g + 1) * STATE]
    tp_start(lambda q: late.at[q], slots_l.at[tp], 2)

    b_all = split(bc_ref[:, 0:half])
    cum_grad = jnp.zeros((rows, heads), F32)
    step_grad = jnp.zeros((rows, heads), F32)
    ends = jnp.zeros((8, heads), F32)
    skips = jnp.zeros((8, heads), F32)
    for cols in tiles(width, size):
        later = pair(later_ref, cols)
        cumx = cumx_ref[:, cols]
        end = cumx[rows - 1 : rows]
        x = x_ref[:, cols]
        dtx = dtx_ref[:, cols]
        dy = dy_ref[:, cols]
        weighted = x * dtx
        from_state = jnp.exp(end - cumx) * mul(b_all, split(block_diagonal(later)))
        dxd = dxd_ref[:, cols] + from_state
        skip = skip_ref[0:1, cols]
        dx = dtx * dxd + skip * dy
        spread = ((iota((heads, size), 1) + cols.start) // HEAD_DIM == iota((heads, size), 0)).astype(F32)
        cum_grad = cum_grad + exact(dy * (y_ref[:, cols] - skip * x) - weighted * dxd, spread, MT)
        step_grad = step_grad + exact(x * dxd, spread, MT)
        end_cols = jnp.sum(weighted * from_state, axis=0, keepdims=True) + jnp.exp(end) * jnp.sum(
            later * pair(enter_ref, cols), axis=0, keepdims=True
        )
        ends = ends + exact(jnp.broadcast_to(end_cols, (8, size)), spread, MT)
        skip_cols = jnp.sum(dy * x, axis=0, keepdims=True)
        skips = skips + exact(jnp.broadcast_to(skip_cols, (8, size)), spread, MT)
        dpre = dx * silu_slope(prex_ref[:, cols])
        dxd_ref[:, cols] = dpre
        for k in range(CONV):
            tap = jnp.sum(dpre * extx[HALO - 3 + k : HALO - 3 + k + rows, cols], axis=0, keepdims=True)
            for i in range(2):
                own_p[cols.start // LANES + i, k : k + 1, :] = tap[:, i * LANES : (i + 1) * LANES]
    send_x = remote(dxd_ref.at[0:8, :], next_x, halo_send.at[2], halo_recv.at[2], behind, tp)

    @pl.when(me > 0)
    def _():
        send_x.start()

    triu = (iota((rows, rows), 0) <= iota((rows, rows), 1)).astype(F32)
    log_grad = exact(triu, cum_grad) + ends[0:1]
    raw_grad = (step_grad - rate * log_grad) * sigmoid(jnp.transpose(dtt_ref[...]) + bias_ref[...])
    ddt_ref[...] = jnp.transpose(raw_grad)
    store(ddt_ref, ddt_hbm)
    small = [
        jnp.sum(raw_grad, axis=0, keepdims=True),
        jnp.sum(-rate * log_grad * step, axis=0, keepdims=True),
        skips[0:1],
    ]
    for i in range(3):
        own_p[i, 5:6, 0:heads] = small[i]

    tp_wait(slots_e, 1)
    tp_wait(slots_l, 2)
    slots_e[tp] = early[tp]
    slots_l[tp] = late[tp]
    both = slots_e[0]
    db = slots_l[0]
    for q in range(1, ranks):
        both = both + slots_e[q]
        db = db + slots_l[q]
    for i, grad in ((0, both[0:rows] + db), (1, both[rows:])):
        mine = pl.ds(pl.multiple_of(i * half + tp * LANES, LANES), LANES)
        dpre = grad * silu_slope(prebc_ref[:, mine])
        dpre_own[i, 0:rows, :] = dpre
        for k in range(CONV):
            own_p[i * CONV + k, 6:7, :] = jnp.sum(
                dpre * extbc[HALO - 3 + k : HALO - 3 + k + rows, mine], axis=0, keepdims=True
            )
    send_bc = remote(dpre_own.at[:, 0:8, :], next_bc, halo_send.at[3], halo_recv.at[3], behind, tp)

    @pl.when(me > 0)
    def _():
        send_bc.start()

    gather_tiles(own_p, slots_p, 4)

    extx[0:rows, :] = dxd_ref[...]

    @pl.when(me < count - 1)
    def _():
        send_x.wait_recv()
        extx[rows : rows + 8, :] = next_x[...]

    @pl.when(me == count - 1)
    def _():
        extx[rows : rows + 8, :] = jnp.zeros((8, width), F32)

    for cols in tiles(width, LANES):
        total = cx_ref[0:1, cols] * extx[3 : 3 + rows, cols]
        for k in range(1, CONV):
            total = total + cx_ref[k : k + 1, cols] * extx[3 - k : 3 - k + rows, cols]
        gx_ref[:, cols] = total.astype(BF16)
    store(gx_ref, gx_hbm)

    def sum_parts():
        slots_p[me] = own_p[my_part]
        for j in range(count):
            slot_wait(slots_p, 4, j)
        total = slots_p[0]
        for j in range(1, count):
            total = total + slots_p[j]
        outs_p[0] = total
        for d in range(1, count):
            from_owner(outs_p.at[0], total_p, 4, lax.rem(me + d, count)).start()
        total_p[my_part] = total

    owner_only(sum_parts)

    @pl.when(me < count - 1)
    def _():
        send_bc.wait_recv()
        dpre_own[:, rows : rows + 8, :] = next_bc[...]

    @pl.when(me == count - 1)
    def _():
        dpre_own[:, rows : rows + 8, :] = jnp.zeros((2, 8, LANES), F32)

    for i in range(2):
        taps = cbc_ref[:, pl.ds(pl.multiple_of(i * half + tp * LANES, LANES), LANES)]
        total = taps[0:1] * dpre_own[i, 3 : 3 + rows, :]
        for k in range(1, CONV):
            total = total + taps[k : k + 1] * dpre_own[i, 3 - k : 3 - k + rows, :]
        final[tp, i * rows : (i + 1) * rows, :] = total.astype(BF16)
    tp_start(lambda q: final.at[tp], final.at[tp], 3)

    settle_exchange(own_p, slots_p, outs_p, total_p, 4)
    for i in range(2 * CONV):
        taps_all[tp, i : i + 1, :] = total_p[i, 6:7, :]
    tp_start(lambda q: taps_all.at[tp], taps_all.at[tp], 4)
    for r, cols in enumerate(tiles(width, LANES)):
        small_ref[:, cols] = total_p[r]
    store(small_ref.at[0:4, :], convx_hbm)
    store(small_ref, small_hbm)

    tp_wait(final, 3)
    for q in range(ranks):
        for i in range(2):
            gbc_ref[i, :, q * STATE : (q + 1) * STATE] = final[q, i * rows : (i + 1) * rows, :]
    store(gbc_ref.at[0], gb_hbm)
    store(gbc_ref.at[1], gc_hbm)
    tp_wait(taps_all, 4)
    for q in range(ranks):
        for i in range(2):
            convbc_ref[i, :, q * STATE : (q + 1) * STATE] = taps_all[q, i * CONV : (i + 1) * CONV, :]
    store(convbc_ref.at[0], convb_hbm)
    store(convbc_ref.at[1], convc_hbm)

    @pl.when(me < count - 1)
    def _():
        for copy in tail:
            copy.wait_send()

    @pl.when(me > 0)
    def _():
        send_x.wait_send()
        send_bc.wait_send()

    drain(own_f, slots_f, outs_f, enter_ref, 0)
    drain(own_b, slots_b, outs_b, later_ref, 2)
    drain(own_p, slots_p, outs_p, total_p, 4)
    for copy in started:
        copy.wait_send()
    for copy in stores:
        copy.wait()


def body(
    x_raw, b_raw, c_raw, z_gate, dt_raw, conv_x, conv_b, conv_c, dt_bias, a_log, d_skip, gain, grad_out
):
    rows, width = x_raw.shape
    heads = dt_raw.shape[1]
    half = b_raw.shape[1]
    count, ranks = lax.axis_size("ctx"), lax.axis_size("tp")
    parts = width // LANES
    hbm = pl.BlockSpec(memory_space=pl.ANY)

    def f32(*shape):
        return pltpu.VMEM(shape, F32)

    def b16(*shape):
        return pltpu.VMEM(shape, BF16)

    full, shared = f32(rows, width), f32(rows, 2 * half)
    outs = [
        ((rows, width), BF16), ((rows, half), BF16), ((rows, half), BF16), ((rows, width), BF16), ((heads, rows), F32),
        ((CONV, width), F32), ((CONV, half), F32), ((CONV, half), F32), ((8, width), F32),
    ]
    scratch = [
        b16(rows, width), b16(rows, 2 * half), b16(rows, width), f32(heads, rows), f32(CONV, width),
        f32(CONV, 2 * half), f32(1, heads), f32(1, heads), f32(1, heads), f32(1, width), b16(rows, width),
        b16(HALO, width + 2 * half), f32(HALO + rows, width), f32(HALO + rows, 2 * half), full, full, shared, shared,
        f32(heads, rows), full, full, f32(8, width),
        full, full, full, f32(GROUPS, rows, rows), f32(GROUPS, rows, rows),
        f32(parts, ROW_F, LANES), f32(count, ROW_F, LANES), f32(count, STATE, LANES), f32(parts, STATE, LANES),
        f32(parts, STATE, LANES), f32(count, STATE, LANES), f32(count, STATE, LANES), f32(parts, STATE, LANES),
        f32(parts, 8, LANES), f32(count, 8, LANES), f32(count, 8, LANES), f32(parts, 8, LANES),
        f32(ranks, 8, rows), f32(ranks, 2 * rows, LANES), f32(ranks, 2 * rows, LANES), f32(ranks, rows, LANES),
        f32(ranks, rows, LANES), b16(ranks, 2 * rows, LANES), f32(ranks, 8, LANES), f32(2, rows + 8, LANES),
        f32(8, width), f32(2, 8, LANES),
        b16(rows, width), b16(2, rows, half), b16(rows, width), f32(heads, rows), f32(2, CONV, half), f32(8, width),
    ] + [
        pltpu.SemaphoreType.DMA(s)
        for s in ((13,), (10,), (6, count), (6, count), (5, ranks), (5, ranks), (4,), (4,))
    ]
    gx, gb, gc, dz, ddt, convx, convb, convc, small = pl.pallas_call(
        mixer_kernel,
        out_shape=[jax.ShapeDtypeStruct(s, d) for s, d in outs],
        in_specs=[hbm] * 13,
        out_specs=[hbm] * len(outs),
        scratch_shapes=scratch,
        compiler_params=pltpu.CompilerParams(
            collective_id=0, has_side_effects=True, vmem_limit_bytes=56 * 1024 * 1024
        ),
    )(
        x_raw, b_raw, c_raw, z_gate, dt_raw.T, conv_x, conv_b, conv_c, dt_bias[None], a_log[None], d_skip[None],
        gain[None], grad_out,
    )
    return (
        gx, gb, gc, dz, ddt.T, convx, convb, convc,
        small[5, :heads], small[5, LANES : LANES + heads], small[5, 2 * LANES : 2 * LANES + heads], small[4],
    )


def solution(mesh):
    col, row, cut = P("ctx", "tp"), P("ctx", None), P("tp")
    return jax.shard_map(
        body,
        mesh=mesh,
        in_specs=(col, row, row, col, col, P(None, "tp"), P(), P(), cut, cut, cut, cut, col),
        out_specs=(col, row, row, col, col, P(None, "tp"), P(), P(), cut, cut, cut, cut),
        check_vma=False,
    )
```

time: 305 us -> 96.2 us (0.32)
  waiting for transfers between devices: 138 us -> 0 us
  blocking collectives: 76.1 us -> 0 us
  Pallas kernels: 23.3 us -> 86 us
  local copies, waits for them, and re-layouts: 44.2 us -> 9.04 us
  between operations: 13.9 us -> 0.67 us
  starting transfers between devices: 7.52 us -> 0 us
    all_gather x2 -> x0, waiting for transfers between devices: 107 us -> none  [the longest x1 66.5 us: body(): state_grads = lax.all_gather(state_part, 'ctx')]
    pallas_call x8 -> x1, Pallas kernels: 23.3 us -> 86 us  [body(): pl.pallas_call(mixer_kernel, out_shape=[jax.ShapeDtypeStruct(s, d) for s,...]
    psum x2 -> x0, blocking collectives: 43.2 us -> none  [the longest x1 37.5 us: body(): packed = lax.psum(packed, 'ctx')]
    all_gather x1 -> x0, blocking collectives: 32.9 us -> none  [body(): decays = lax.all_gather(dec, 'ctx')]
    unnamed x104 -> x22, local copies, waits for them, and re-layouts: 37.2 us -> 6.48 us
    psum x1 -> x0, waiting for transfers between devices: 27 us -> none  [body(): dbc = lax.psum(dbc, 'tp')]
    ppermute x3 -> x0, starting transfers between devices: 7.4 us -> none  [the longest x1 4.84 us: body(): halo = lax.ppermute(tails, 'ctx', [(i, i + 1) for i in range(count - 1)])]
    slice x10 -> x1, local copies, waits for them, and re-layouts: 6.05 us -> 1.35 us  [body(): small[4]]
  transfers between devices with their start and end apart: 6 -> 0, of which waited for: 5 -> 0; matrix products, arithmetic and copies ran while one was open for 3% -> 0% of each run, Pallas kernels for 2% -> 0%
where the time goes in v2:
time: 96.2 us; the launch traced here: 95.7 us
  Pallas kernels  86 us (89%)
  local copies, waits for them, and re-layouts  9.04 us (9%)
    pallas_call x1, Pallas kernels, body(): pl.pallas_call(mixer_kernel, out_shape=[jax.ShapeDtypeStruct(s, d) for s,...  86 us
    unnamed x22, local copies, waits for them, and re-layouts  6.48 us

profile of v2, /device:TPU:0, one launch (start us, length us, event | category | flops | bytes accessed | tf_op | source)
XLA Modules:
  0.0 95.7 jit_solution(17926372979194999285)
XLA Ops:
  0.6 86.0 %shard_map.220 = (bf16[128,1024]{1,0:T(8,128)(2,1)}, bf16[128,512]{1,0:T(8,128)(2,1)}, bf16[128,512]{1,0:T(8,128)(2,1)}, bf16[128,1024]{1,0:T(8,128)(2,1)}, f32[...) custom-call(bf16[128,1024]{1,0:T(8,128)(2,1)} %x_hbm.1, ...), custom_call_target="tpu_custom_call" | custom-call | tf_op jit(solution)/shard_map/pallas_call | solution.py:620
  86.6 1.2 %slice_bitcast_fusion = (f32[32]{0:T(128)}, f32[32]{0:T(128)}, f32[32]{0:T(128)}) fusion(f32[8,1024]{1,0:T(8,128)} %get-tuple-element.29), kind=kLoop, calls=%fused_computation | loop fusion | bytes 768 | tf_op jit(solution)/shard_map/squeeze | solution.py:635
  87.8 1.4 %slice.15 = f32[1,1024]{1,0:T(1,128)} slice(f32[8,1024]{1,0:T(8,128)} %get-tuple-element.29), slice={[4:5], [0:1024]} | slice | bytes 8192 | tf_op jit(solution)/shard_map/slice | solution.py:635
  89.2 0.0 copy-start.2
  89.2 0.0 copy-start.1
  89.2 1.7 %copy.33 = bf16[128,1024]{1,0:T(8,128)(2,1)} copy(bf16[128,1024]{1,0:T(8,128)(2,1)} %get-tuple-element.45) | data formatting | bytes 524288
  90.9 0.0 copy-done.2
  90.9 0.0 copy-start
  90.9 0.7 copy.34
  91.6 0.0 copy-done.1
  91.6 0.7 copy.35
  92.2 0.0 copy-done
  92.2 0.0 copy-start.4
  92.2 0.7 copy.36
  92.9 0.0 copy-done.4
  93.0 0.0 copy-start.3
  93.0 0.6 copy.37
  93.6 0.1 copy-done.3
  93.7 0.0 copy-start.6
  93.7 0.6 copy.38
  94.3 0.1 copy-done.6
  94.4 0.0 copy-start.5
  94.4 0.6 copy.39
  95.0 0.1 copy-done.5
  95.1 0.6 copy.40
Async XLA Ops:
  89.2 1.7 %copy-start.2 = (bf16[128,512]{1,0:T(8,128)(2,1)S(1)}, bf16[128,512]{1,0:T(8,128)(2,1)}, u32[]{:S(2)}) copy-start(bf16[128,512]{1,0:T(8,128)(2,1)} %get-tuple-element.46) | copy-start | bytes 393220
  89.2 2.4 %copy-start.1 = (bf16[128,512]{1,0:T(8,128)(2,1)S(1)}, bf16[128,512]{1,0:T(8,128)(2,1)}, u32[]{:S(2)}) copy-start(bf16[128,512]{1,0:T(8,128)(2,1)} %get-tuple-element.47) | copy-start | bytes 393220
  90.9 1.3 %copy-start = (bf16[128,1024]{1,0:T(8,128)(2,1)S(1)}, bf16[128,1024]{1,0:T(8,128)(2,1)}, u32[]{:S(2)}) copy-start(bf16[128,1024]{1,0:T(8,128)(2,1)} %get-tuple-element.48) | copy-start | bytes 786436
  92.2 0.7 copy-start.4
  93.0 0.7 copy-start.3
  93.7 0.7 copy-start.6
  94.4 0.7 copy-start.5

commit v3 on v2

--- a/solution.py
+++ b/solution.py
@@ -91,14 +91,14 @@
 
 def mixer_kernel(
     x_hbm, b_hbm, c_hbm, z_hbm, dtt_hbm, cx_hbm, cb_hbm, cc_hbm, bias_hbm, alog_hbm, dskip_hbm, gain_hbm, go_hbm,
-    gx_hbm, gb_hbm, gc_hbm, dz_hbm, ddt_hbm, convx_hbm, convb_hbm, convc_hbm, small_hbm,
+    gx_hbm, gb_hbm, gc_hbm, dz_hbm, ddt_hbm, convx_hbm, convb_hbm, convc_hbm, bias_out, alog_out, skip_out, gain_out,
     x_in, bc_in, z_ref, dtt_ref, cx_ref, cbc_ref, bias_ref, alog_ref, dskip_ref, gain_ref, go_ref,
     halo_ref, extx, extbc, prex_ref, x_ref, prebc_ref, bc_ref, cumt_ref, dtx_ref, cumx_ref, skip_ref,
     y_ref, dy_ref, dxd_ref, inner, inner_grad,
-    own_f, slots_f, outs_f, enter_ref, own_b, slots_b, outs_b, later_ref,
-    own_p, slots_p, outs_p, total_p,
+    own_f, pair_f, chain_in_f, chain_out_f, back_f, enter_ref, own_b, pair_b, chain_in_b, chain_out_b, back_b, later_ref,
+    own_p, slots_p, outs_p, total_p, taps_slots,
     sums_slots, early, slots_e, late, slots_l, final, taps_all, dpre_own, next_x, next_bc,
-    gx_ref, gbc_ref, dz_ref, ddt_ref, convbc_ref, small_ref,
+    gx_ref, gbc_ref, dz_ref, ddt_ref, convbc_ref, small_ref, bias_sum, alog_sum, skip_sum, gain_sum,
     load_sem, store_sem, ctx_send, ctx_recv, tp_send, tp_recv, halo_send, halo_recv,
 ):
     me, tp = lax.axis_index("ctx"), lax.axis_index("tp")
@@ -245,35 +245,91 @@
             for i in range(count):
                 @pl.when(me != i)
                 def _():
-                    from_owner(outs.at[i], result, k, i).wait_send()
+                    from_owner(outs.at[0], result, k, i).wait_send()
 
         owner_only(sent)
 
-    def scan(own, slots, decays, outs, result, k, order):
-        def act():
-            slots[me] = own[my_part]
-            total = jnp.zeros((STATE, LANES), F32)
-            for i in order:
-                outs[i] = total
-
-                @pl.when(i != me)
-                def _():
-                    from_owner(outs.at[i], result, k, i).start()
-
-                slot_wait(slots, k, i)
-                total = decays[i, STATE : STATE + 1, :] * total + slots[i, 0:STATE, :]
-            result[my_part] = outs[me]
-
-        owner_only(act)
-
-    gather_tiles(own_f, slots_f, 0)
+    side = lax.rem(me, 2)
+    partner = me + 1 - 2 * side
+    half_parts = parts // 2
+
+    def to_partner(own, pair_in, row, k):
+        return remote(
+            own.at[(1 - side) * half_parts + k], pair_in.at[k], ctx_send.at[row, k], ctx_recv.at[row, k], partner, tp
+        )
+
+    def to_next(chain_out, chain_in, row, k, there):
+        return remote(chain_out.at[k], chain_in.at[k], ctx_send.at[row + 2, k], ctx_recv.at[row + 2, k], there, tp)
+
+    def hand_back(back, result, row, k, part):
+        return remote(back.at[k], result.at[part], ctx_send.at[row + 1, k], ctx_recv.at[row + 1, k], partner, tp)
+
+    def swap_halves(own, pair_in, row):
+        for k in range(half_parts):
+            to_partner(own, pair_in, row, k).start()
+
+    def pair_scan(own, pair_in, chain_in, chain_out, back, result, row, backward, between):
+        if backward:
+            there, has_prev, has_next, leads = lax.rem(me + count - 2, count), me < count - 2, me >= 2, side == 1
+        else:
+            there, has_prev, has_next, leads = lax.rem(me + 2, count), me >= 2, me < count - 2, side == 0
+        for k in range(half_parts):
+            part = side * half_parts + k
+            to_partner(own, pair_in, row, k).wait_recv()
+            mine, other = own[part], pair_in[k]
+            mine_decay, other_decay = own_f[part][STATE : STATE + 1], pair_f[k][STATE : STATE + 1]
+            first = jnp.where(leads, mine[0:STATE], other[0:STATE])
+            second = jnp.where(leads, other[0:STATE], mine[0:STATE])
+            first_decay = jnp.where(leads, mine_decay, other_decay)
+            second_decay = jnp.where(leads, other_decay, mine_decay)
+
+            @pl.when(has_prev)
+            def _():
+                to_next(chain_out, chain_in, row, k, there).wait_recv()
+
+            @pl.when(jnp.logical_not(has_prev))
+            def _():
+                chain_in[k] = jnp.zeros((STATE, LANES), F32)
+
+            coming = chain_in[k]
+            middle = first_decay * coming + first
+
+            @pl.when(has_next)
+            def _():
+                chain_out[k] = second_decay * middle + second
+                to_next(chain_out, chain_in, row, k, there).start()
+
+            result[part] = jnp.where(leads, coming, middle)
+            back[k] = jnp.where(leads, middle, coming)
+            hand_back(back, result, row, k, part).start()
+            between(k)
+
+        def finish():
+            for k in range(half_parts):
+                hand_back(back, result, row, k, (1 - side) * half_parts + k).wait_recv()
+
+        def drain_scan():
+            for k in range(half_parts):
+                to_partner(own, pair_in, row, k).wait_send()
+                hand_back(back, result, row, k, side * half_parts + k).wait_send()
+
+            @pl.when(has_next)
+            def _():
+                for k in range(half_parts):
+                    to_next(chain_out, chain_in, row, k, there).wait_send()
+
+        return finish, drain_scan
+
+    swap_halves(own_f, pair_f, 0)
 
     owner = lane_group(LANES)
     causal = iota((rows, rows), 0) >= iota((rows, rows), 1)
     for g in range(GROUPS):
         c_g = split(bc_ref[:, half + g * STATE : half + (g + 1) * STATE])
         inner[g] = mul(c_g, split(bc_ref[:, g * STATE : (g + 1) * STATE]), MT)
-    for r, cols in enumerate(tiles(width, LANES)):
+
+    def inside(r):
+        cols = slice(r * LANES, (r + 1) * LANES)
         x = x_ref[:, cols]
         weighted = x * dtx_ref[:, cols]
         cumx = cumx_ref[:, cols]
@@ -285,10 +341,16 @@
             total = total + mul(split(fade), split(jnp.where(owner == g, weighted, 0.0)))
         y_ref[:, cols] = total
 
-    scan(own_f, slots_f, slots_f, outs_f, enter_ref, 0, range(count))
+    def two_inside(k):
+        inside(2 * k)
+        inside(2 * k + 1)
+
+    finish_f, drain_f = pair_scan(
+        own_f, pair_f, chain_in_f, chain_out_f, back_f, enter_ref, 0, False, two_inside
+    )
     for copy in loads[11:]:
         copy.wait()
-    settle_exchange(own_f, slots_f, outs_f, enter_ref, 0)
+    finish_f()
 
     c_all = split(bc_ref[:, half:])
     squares = jnp.zeros((rows, LANES), F32)
@@ -359,7 +421,7 @@
             part = slice(i * LANES, (i + 1) * LANES)
             own_b[cols.start // LANES + i] = state[:, part]
             own_p[cols.start // LANES + i, 4:5, :] = gain_grad[:, part]
-    gather_tiles(own_b, slots_b, 2)
+    swap_halves(own_b, pair_b, 3)
 
     stores = []
 
@@ -374,8 +436,16 @@
         c_g = split(bc_ref[:, half + g * STATE : half + (g + 1) * STATE])
         inner[g] = mul(split(bc_ref[:, g * STATE : (g + 1) * STATE]), c_g, MT)
     inner_grad[...] = jnp.zeros_like(inner_grad)
-    causal = iota((rows, rows), 0) <= iota((rows, rows), 1)
-    for r, cols in enumerate(tiles(width, LANES)):
+    causal_back = iota((rows, rows), 0) <= iota((rows, rows), 1)
+    dc = jnp.zeros((rows, half), F32)
+    for cols in tiles(width, size):
+        pushed = jnp.exp(cumx_ref[:, cols]) * dy_ref[:, cols]
+        dc = dc + mul(split(pushed), split(block_diagonal(pair(enter_ref, cols))), MT)
+    for g in range(GROUPS):
+        early[g, rows:, :] = dc[:, g * STATE : (g + 1) * STATE]
+
+    def inside_back(r):
+        cols = slice(r * LANES, (r + 1) * LANES)
         dy = dy_ref[:, cols]
         cumx = cumx_ref[:, cols]
         weighted = split(x_ref[:, cols] * dtx_ref[:, cols])
@@ -383,25 +453,28 @@
         for g in range(GROUPS):
             h = r * GROUPS + g
             gap = cumt_ref[h : h + 1, :] - cumx[:, g * HEAD_DIM : g * HEAD_DIM + 1]
-            decay = jnp.exp(jnp.where(causal, gap, -1e30))
+            decay = jnp.exp(jnp.where(causal_back, gap, -1e30))
             masked = split(jnp.where(owner == g, dy, 0.0))
             total = total + mul(split(decay * inner[g]), masked)
             inner_grad[g] = inner_grad[g] + decay * mul(weighted, masked, MT)
         dxd_ref[:, cols] = total
-    dc = jnp.zeros((rows, half), F32)
-    for cols in tiles(width, size):
-        pushed = jnp.exp(cumx_ref[:, cols]) * dy_ref[:, cols]
-        dc = dc + mul(split(pushed), split(block_diagonal(pair(enter_ref, cols))), MT)
+
+    def two_inside_back(k):
+        inside_back(2 * k)
+        inside_back(2 * k + 1)
+
+    finish_b, drain_b = pair_scan(
+        own_b, pair_b, chain_in_b, chain_out_b, back_b, later_ref, 3, True, two_inside_back
+    )
     for g in range(GROUPS):
         own = slice(g * STATE, (g + 1) * STATE)
         other = slice(half + g * STATE, half + (g + 1) * STATE)
         grad = inner_grad[g]
         early[g, 0:rows, :] = mul(split(grad), split(bc_ref[:, other]))
-        early[g, rows:, :] = dc[:, own] + mul(split(jnp.transpose(grad)), split(bc_ref[:, own]))
+        early[g, rows:, :] = early[g, rows:, :] + mul(split(jnp.transpose(grad)), split(bc_ref[:, own]))
     tp_start(lambda q: early.at[q], slots_e.at[tp], 1)
 
-    scan(own_b, slots_b, slots_f, outs_b, later_ref, 2, range(count - 1, -1, -1))
-    settle_exchange(own_b, slots_b, outs_b, later_ref, 2)
+    finish_b()
 
     db = jnp.zeros((rows, half), F32)
     for cols in tiles(width, size):
@@ -464,6 +537,7 @@
     for i in range(3):
         own_p[i, 5:6, 0:heads] = small[i]
 
+    gather_tiles(own_p, slots_p, 6)
     tp_wait(slots_e, 1)
     tp_wait(slots_l, 2)
     slots_e[tp] = early[tp]
@@ -478,7 +552,7 @@
         dpre = grad * silu_slope(prebc_ref[:, mine])
         dpre_own[i, 0:rows, :] = dpre
         for k in range(CONV):
-            own_p[i * CONV + k, 6:7, :] = jnp.sum(
+            taps_slots[me, i * CONV + k : i * CONV + k + 1, :] = jnp.sum(
                 dpre * extbc[HALO - 3 + k : HALO - 3 + k + rows, mine], axis=0, keepdims=True
             )
     send_bc = remote(dpre_own.at[:, 0:8, :], next_bc, halo_send.at[3], halo_recv.at[3], behind, tp)
@@ -487,7 +561,11 @@
     def _():
         send_bc.start()
 
-    gather_tiles(own_p, slots_p, 4)
+    def to_all(i):
+        return remote(taps_slots.at[me], taps_slots.at[me], ctx_send.at[8, i], ctx_recv.at[8, me], i, tp)
+
+    for d in range(1, count):
+        to_all(lax.rem(me + d, count)).start()
 
     extx[0:rows, :] = dxd_ref[...]
 
@@ -510,13 +588,13 @@
     def sum_parts():
         slots_p[me] = own_p[my_part]
         for j in range(count):
-            slot_wait(slots_p, 4, j)
+            slot_wait(slots_p, 6, j)
         total = slots_p[0]
         for j in range(1, count):
             total = total + slots_p[j]
         outs_p[0] = total
         for d in range(1, count):
-            from_owner(outs_p.at[0], total_p, 4, lax.rem(me + d, count)).start()
+            from_owner(outs_p.at[0], total_p, 6, lax.rem(me + d, count)).start()
         total_p[my_part] = total
 
     owner_only(sum_parts)
@@ -538,14 +616,26 @@
         final[tp, i * rows : (i + 1) * rows, :] = total.astype(BF16)
     tp_start(lambda q: final.at[tp], final.at[tp], 3)
 
-    settle_exchange(own_p, slots_p, outs_p, total_p, 4)
-    for i in range(2 * CONV):
-        taps_all[tp, i : i + 1, :] = total_p[i, 6:7, :]
+    for j in range(count):
+        slot_wait(taps_slots, 8, j)
+    taps_sum = taps_slots[0]
+    for j in range(1, count):
+        taps_sum = taps_sum + taps_slots[j]
+    taps_all[tp] = taps_sum
     tp_start(lambda q: taps_all.at[tp], taps_all.at[tp], 4)
+
+    settle_exchange(own_p, slots_p, outs_p, total_p, 6)
     for r, cols in enumerate(tiles(width, LANES)):
-        small_ref[:, cols] = total_p[r]
-    store(small_ref.at[0:4, :], convx_hbm)
-    store(small_ref, small_hbm)
+        small_ref[:, cols] = total_p[r, 0:CONV, :]
+        gain_sum[:, cols] = total_p[r, 4:5, :]
+    bias_sum[...] = total_p[0, 5:6, 0:heads]
+    alog_sum[...] = total_p[1, 5:6, 0:heads]
+    skip_sum[...] = total_p[2, 5:6, 0:heads]
+    store(small_ref, convx_hbm)
+    store(gain_sum, gain_out)
+    store(bias_sum, bias_out)
+    store(alog_sum, alog_out)
+    store(skip_sum, skip_out)
 
     tp_wait(final, 3)
     for q in range(ranks):
@@ -570,12 +660,24 @@
         send_x.wait_send()
         send_bc.wait_send()
 
-    drain(own_f, slots_f, outs_f, enter_ref, 0)
-    drain(own_b, slots_b, outs_b, later_ref, 2)
-    drain(own_p, slots_p, outs_p, total_p, 4)
+    drain_f()
+    drain_b()
+    drain(own_p, slots_p, outs_p, total_p, 6)
+    for d in range(1, count):
+        to_all(lax.rem(me + d, count)).wait_send()
     for copy in started:
         copy.wait_send()
     for copy in stores:
+        copy.wait()
+
+
+def deliver_kernel(*refs):
+    number = len(refs) // 2
+    sem = refs[-1]
+    copies = [pltpu.make_async_copy(refs[i], refs[number + i], sem.at[i]) for i in range(number)]
+    for copy in copies:
+        copy.start()
+    for copy in copies:
         copy.wait()
 
 
@@ -598,7 +700,8 @@
     full, shared = f32(rows, width), f32(rows, 2 * half)
     outs = [
         ((rows, width), BF16), ((rows, half), BF16), ((rows, half), BF16), ((rows, width), BF16), ((heads, rows), F32),
-        ((CONV, width), F32), ((CONV, half), F32), ((CONV, half), F32), ((8, width), F32),
+        ((CONV, width), F32), ((CONV, half), F32), ((CONV, half), F32), ((1, heads), F32), ((1, heads), F32),
+        ((1, heads), F32), ((1, width), F32),
     ]
     scratch = [
         b16(rows, width), b16(rows, 2 * half), b16(rows, width), f32(heads, rows), f32(CONV, width),
@@ -606,20 +709,23 @@
         b16(HALO, width + 2 * half), f32(HALO + rows, width), f32(HALO + rows, 2 * half), full, full, shared, shared,
         f32(heads, rows), full, full, f32(8, width),
         full, full, full, f32(GROUPS, rows, rows), f32(GROUPS, rows, rows),
-        f32(parts, ROW_F, LANES), f32(count, ROW_F, LANES), f32(count, STATE, LANES), f32(parts, STATE, LANES),
-        f32(parts, STATE, LANES), f32(count, STATE, LANES), f32(count, STATE, LANES), f32(parts, STATE, LANES),
-        f32(parts, 8, LANES), f32(count, 8, LANES), f32(count, 8, LANES), f32(parts, 8, LANES),
+        f32(parts, ROW_F, LANES), f32(parts // 2, ROW_F, LANES), *[f32(parts // 2, STATE, LANES)] * 3,
+        f32(parts, STATE, LANES),
+        f32(parts, STATE, LANES), *[f32(parts // 2, STATE, LANES)] * 4, f32(parts, STATE, LANES),
+        f32(parts, 8, LANES), f32(count, 8, LANES), f32(1, 8, LANES), f32(parts, 8, LANES), f32(count, 8, LANES),
         f32(ranks, 8, rows), f32(ranks, 2 * rows, LANES), f32(ranks, 2 * rows, LANES), f32(ranks, rows, LANES),
         f32(ranks, rows, LANES), b16(ranks, 2 * rows, LANES), f32(ranks, 8, LANES), f32(2, rows + 8, LANES),
         f32(8, width), f32(2, 8, LANES),
-        b16(rows, width), b16(2, rows, half), b16(rows, width), f32(heads, rows), f32(2, CONV, half), f32(8, width),
+        b16(rows, width), b16(2, rows, half), b16(rows, width), f32(heads, rows), f32(2, CONV, half), f32(CONV, width),
+        f32(1, heads), f32(1, heads), f32(1, heads), f32(1, width),
     ] + [
         pltpu.SemaphoreType.DMA(s)
-        for s in ((13,), (10,), (6, count), (6, count), (5, ranks), (5, ranks), (4,), (4,))
+        for s in ((13,), (12,), (9, count), (9, count), (5, ranks), (5, ranks), (4,), (4,))
     ]
-    gx, gb, gc, dz, ddt, convx, convb, convc, small = pl.pallas_call(
+    shapes = [jax.ShapeDtypeStruct(s, d) for s, d in outs]
+    results = pl.pallas_call(
         mixer_kernel,
-        out_shape=[jax.ShapeDtypeStruct(s, d) for s, d in outs],
+        out_shape=shapes,
         in_specs=[hbm] * 13,
         out_specs=[hbm] * len(outs),
         scratch_shapes=scratch,
@@ -630,10 +736,15 @@
         x_raw, b_raw, c_raw, z_gate, dt_raw.T, conv_x, conv_b, conv_c, dt_bias[None], a_log[None], d_skip[None],
         gain[None], grad_out,
     )
-    return (
-        gx, gb, gc, dz, ddt.T, convx, convb, convc,
-        small[5, :heads], small[5, LANES : LANES + heads], small[5, 2 * LANES : 2 * LANES + heads], small[4],
-    )
+    gx, gb, gc, dz, ddt, convx, convb, convc, bias, alog, skip, gain_grad = pl.pallas_call(
+        deliver_kernel,
+        out_shape=shapes,
+        in_specs=[hbm] * len(outs),
+        out_specs=[hbm] * len(outs),
+        scratch_shapes=[pltpu.SemaphoreType.DMA((len(outs),))],
+        compiler_params=pltpu.CompilerParams(vmem_limit_bytes=56 * 1024 * 1024),
+    )(*results)
+    return gx, gb, gc, dz, ddt.T, convx, convb, convc, bias[0], alog[0], skip[0], gain_grad[0]
 
 
 def solution(mesh):

time: 96.2 us -> 103 us (1.071)
  Pallas kernels: 86 us -> 102 us
  local copies, waits for them, and re-layouts: 9.04 us -> 0 us
    pallas_call x1 -> x2, Pallas kernels: 86 us -> 102 us  [the longest x1 75.7 us: body(): pl.pallas_call(mixer_kernel, out_shape=shapes, in_specs=[hbm] * 13, out_s...]
    unnamed x22 -> x0, local copies, waits for them, and re-layouts: 6.48 us -> none
    slice x1 -> x0, local copies, waits for them, and re-layouts: 1.35 us -> none  [body(): small[4]]
    squeeze x1 -> x0, local copies, waits for them, and re-layouts: 1.21 us -> none  [body(): small[5, 2 * LANES:2 * LANES + heads]]
where the time goes in v3:
time: 103 us
  Pallas kernels  102 us (99%)
    pallas_call x1, Pallas kernels, body(): pl.pallas_call(mixer_kernel, out_shape=shapes, in_specs=[hbm] * 13, out_s...  75.7 us
    pallas_call x1, Pallas kernels, body(): pl.pallas_call(deliver_kernel, out_shape=shapes, in_specs=[hbm] * len(out...  26.7 us

profile of v3, /device:TPU:0, one launch (start us, length us, event | category | flops | bytes accessed | tf_op | source)
XLA Modules:
  0.0 103.2 jit_solution(16289560266003147698)
XLA Ops:
  0.6 75.7 %shard_map.220 = (bf16[128,1024]{1,0:T(8,128)(2,1)}, bf16[128,512]{1,0:T(8,128)(2,1)}, bf16[128,512]{1,0:T(8,128)(2,1)}, bf16[128,1024]{1,0:T(8,128)(2,1)}, f32[...) custom-call(bf16[128,1024]{1,0:T(8,128)(2,1)} %x_hbm.1, ...), custom_call_target="tpu_custom_call" | custom-call | tf_op jit(solution)/shard_map/pallas_call | solution.py:726
  76.3 26.7 %shard_map.221 = (bf16[128,1024]{1,0:T(8,128)(2,1)}, bf16[128,512]{1,0:T(8,128)(2,1)}, bf16[128,512]{1,0:T(8,128)(2,1)}, bf16[128,1024]{1,0:T(8,128)(2,1)}, f32[...) custom-call(bf16[128,1024]{1,0:T(8,128)(2,1)} %get-tuple-element.36., ...), custom_call_target="tpu_custom_call" | custom-call | tf_op jit(solution)/shard_map/pallas_call | solution.py:739

commit v4 on v3

--- a/solution.py
+++ b/solution.py
@@ -1,3 +1,5 @@
+import functools
+
 import jax
 import jax.numpy as jnp
 from jax import lax
@@ -671,13 +673,17 @@
         copy.wait()
 
 
-def deliver_kernel(*refs):
-    number = len(refs) // 2
-    sem = refs[-1]
-    copies = [pltpu.make_async_copy(refs[i], refs[number + i], sem.at[i]) for i in range(number)]
-    for copy in copies:
+def deliver_kernel(number, *refs):
+    held = refs[2 * number : 3 * number]
+    arrive, leave = refs[3 * number :]
+    incoming = [pltpu.make_async_copy(refs[i], held[i], arrive.at[i]) for i in range(number)]
+    outgoing = [pltpu.make_async_copy(held[i], refs[number + i], leave.at[i]) for i in range(number)]
+    for copy in incoming:
         copy.start()
-    for copy in copies:
+    for arrived, copy in zip(incoming, outgoing):
+        arrived.wait()
+        copy.start()
+    for copy in outgoing:
         copy.wait()
 
 
@@ -737,11 +743,11 @@
         gain[None], grad_out,
     )
     gx, gb, gc, dz, ddt, convx, convb, convc, bias, alog, skip, gain_grad = pl.pallas_call(
-        deliver_kernel,
+        functools.partial(deliver_kernel, len(outs)),
         out_shape=shapes,
         in_specs=[hbm] * len(outs),
         out_specs=[hbm] * len(outs),
-        scratch_shapes=[pltpu.SemaphoreType.DMA((len(outs),))],
+        scratch_shapes=[pltpu.VMEM(s, d) for s, d in outs] + [pltpu.SemaphoreType.DMA((len(outs),))] * 2,
         compiler_params=pltpu.CompilerParams(vmem_limit_bytes=56 * 1024 * 1024),
     )(*results)
     return gx, gb, gc, dz, ddt.T, convx, convb, convc, bias[0], alog[0], skip[0], gain_grad[0]

time: 103 us -> 78.8 us (0.77)
  Pallas kernels: 102 us -> 77.8 us
    pallas_call x1, Pallas kernels: 26.7 us -> 2.09 us  [body(): pl.pallas_call(functools.partial(deliver_kernel, len(outs)), out_shape=sh...]
where the time goes in v4:
time: 78.8 us; the launch traced here: 78.6 us
  Pallas kernels  77.8 us (99%)
  between operations  0.82 us (1%)
    pallas_call x1, Pallas kernels, body(): pl.pallas_call(mixer_kernel, out_shape=shapes, in_specs=[hbm] * 13, out_s...  75.7 us
    pallas_call x1, Pallas kernels, body(): pl.pallas_call(functools.partial(deliver_kernel, len(outs)), out_shape=sh...  2.09 us

profile of v4, /device:TPU:0, one launch (start us, length us, event | category | flops | bytes accessed | tf_op | source)
XLA Modules:
  0.0 78.6 jit_solution(509237985919036984)
XLA Ops:
  0.6 75.7 %shard_map.220 = (bf16[128,1024]{1,0:T(8,128)(2,1)}, bf16[128,512]{1,0:T(8,128)(2,1)}, bf16[128,512]{1,0:T(8,128)(2,1)}, bf16[128,1024]{1,0:T(8,128)(2,1)}, f32[...) custom-call(bf16[128,1024]{1,0:T(8,128)(2,1)} %x_hbm.1, ...), custom_call_target="tpu_custom_call" | custom-call | tf_op jit(solution)/shard_map/pallas_call | solution.py:732
  76.3 2.1 %shard_map.221 = (bf16[128,1024]{1,0:T(8,128)(2,1)}, bf16[128,512]{1,0:T(8,128)(2,1)}, bf16[128,512]{1,0:T(8,128)(2,1)}, bf16[128,1024]{1,0:T(8,128)(2,1)}, f32[...) custom-call(bf16[128,1024]{1,0:T(8,128)(2,1)} %get-tuple-element.36., ...), custom_call_target="tpu_custom_call" | custom-call | tf_op jit(solution)/shard_map/pallas_call | solution.py:745
